TPU v7x, 256 devices: a whole 4x4x8 slice. The times are simulated.
256 devices in a mesh: grp: 4 (over y), ep: 64 (over x, z, core).
Axes of the slice: x: 4, y: 4, z: 8, core: 2. Of those that a mesh axis runs over, the one named last changes fastest.
Arguments:
- tokens: bfloat16 [8192, 2048], P(('grp', 'ep')), may hold values from -6 to 6
- grad_out: bfloat16 [8192, 2048], P(('grp', 'ep')), may hold values from -0.29882812 to 0.29882812
- combine: bfloat16 [8192, 10], P(('grp', 'ep')), may hold values from 0.19921875 to 1.5
- expert_ids: int32 [8192, 10], P(('grp', 'ep')), may hold values from 0 to 63, all different within a row; in each aligned block of 32 rows (0 to 31, 32 to 63, ...) at most 16 rows name the same one
- w_gate: bfloat16 [64, 2048, 512], P('ep'), may hold values from -0.125 to 0.125
- w_up: bfloat16 [64, 2048, 512], P('ep'), may hold values from -0.125 to 0.125
- w_down: bfloat16 [64, 512, 2048], P('ep'), may hold values from -0.25 to 0.25
Outputs:
- grad_tokens: bfloat16 [8192, 2048], P(('grp', 'ep'))
- grad_combine: bfloat16 [8192, 10], P(('grp', 'ep'))
- grad_gate: bfloat16 [64, 2048, 512], P('ep', 'grp')
- grad_up: bfloat16 [64, 2048, 512], P('ep', 'grp')
- grad_down: bfloat16 [64, 512, 2048], P('ep', None, 'grp')
Inputs may be any that keep to these rules, and one draw needn't show every extreme that they name: `expert_ids`: each row names 10 different experts. Within the rows of one device (aligned blocks of 32 rows) no expert is named by more than 16 rows, and in some block one expert is named by exactly 16 rows.
All inputs are finite; a program needn't handle non-finite values.
Results may differ from a plain program's by a relative error of at most 0.013.
Values may be sent and summed in bfloat16 or wider, within the bound.
A program may use at most 128 MiB of HBM per device.

v0:
```python
import jax
import jax.numpy as jnp
from jax import lax
from jax.sharding import PartitionSpec as P

row_block = 128


def dot_plain(left, right):
    return jnp.dot(left, right, preferred_element_type=jnp.float32)


def dot_back(left, right):
    return lax.dot_general(
        left, right, (((1,), (1,)), ((), ())), preferred_element_type=jnp.float32
    )


def dot_rows(left, right):
    return lax.dot_general(
        left, right, (((0,), (0,)), ((), ())), preferred_element_type=jnp.float32
    )


def expert_rows(rows_x, rows_dy, rows_w, gate_weight, up_weight, down_weight):
    pre_gate = dot_plain(rows_x, gate_weight)
    pre_up = dot_plain(rows_x, up_weight)
    sigmoid_gate = jax.nn.sigmoid(pre_gate)
    activation = pre_gate * sigmoid_gate
    derivative = sigmoid_gate * (1.0 + pre_gate * (1.0 - sigmoid_gate))
    hidden = (activation * pre_up).astype(jnp.bfloat16)
    output = dot_plain(hidden, down_weight)
    weight_grad = jnp.sum(rows_dy.astype(jnp.float32) * output, axis=1)
    scaled = (rows_w.astype(jnp.float32)[:, None] * rows_dy.astype(jnp.float32)).astype(
        jnp.bfloat16
    )
    grad_hidden = dot_back(scaled, down_weight)
    up_rows = (grad_hidden * activation).astype(jnp.bfloat16)
    gate_rows = (grad_hidden * pre_up * derivative).astype(jnp.bfloat16)
    grad_rows = (dot_back(gate_rows, gate_weight) + dot_back(up_rows, up_weight)).astype(
        jnp.bfloat16
    )
    return (hidden, scaled, gate_rows, up_rows, grad_rows, weight_grad)


def owner_blocks(recv_x, recv_dy, recv_w, gate_weight, up_weight, down_weight):
    sources, capacity, row_width = recv_x.shape
    slot_count = sources * capacity
    live_mask = recv_w != 0
    counts = jnp.sum(live_mask.astype(jnp.int32), axis=1)
    run_ends = jnp.cumsum(counts)
    starts = run_ends - counts
    live_total = jnp.sum(counts)
    dense_pos = jnp.arange(slot_count, dtype=jnp.int32)
    before_mask = (dense_pos[:, None] >= run_ends[None, :]).astype(jnp.int32)
    source_of = jnp.minimum(jnp.sum(before_mask, axis=1), sources - 1)
    slot_of = dense_pos - jnp.sum(before_mask * counts[None, :], axis=1)
    is_valid = dense_pos < live_total
    pick_row = jnp.where(is_valid, source_of * capacity + slot_of, 0)
    dense_x = jnp.where(
        is_valid[:, None],
        recv_x.reshape(slot_count, row_width)[pick_row],
        jnp.zeros((), jnp.bfloat16),
    )
    dense_dy = jnp.where(
        is_valid[:, None],
        recv_dy.reshape(slot_count, row_width)[pick_row],
        jnp.zeros((), jnp.bfloat16),
    )
    dense_w = jnp.where(is_valid, recv_w.reshape(slot_count)[pick_row], jnp.zeros((), jnp.bfloat16))
    block_rows = min(row_block, slot_count)
    nblocks = (live_total + block_rows - 1) // block_rows

    def block_step(block_index, carried):
        dense_dx, dense_gk, acc_gate, acc_up, acc_down = carried
        first_row = block_index * block_rows
        part_x = lax.dynamic_slice_in_dim(dense_x, first_row, block_rows, 0)
        part_dy = lax.dynamic_slice_in_dim(dense_dy, first_row, block_rows, 0)
        part_w = lax.dynamic_slice_in_dim(dense_w, first_row, block_rows, 0)
        hidden, scaled, gate_rows, up_rows, grad_rows, weight_grad = expert_rows(
            part_x, part_dy, part_w, gate_weight, up_weight, down_weight
        )
        dense_dx = lax.dynamic_update_slice_in_dim(dense_dx, grad_rows, first_row, 0)
        dense_gk = lax.dynamic_update_slice_in_dim(dense_gk, weight_grad, first_row, 0)
        return (
            dense_dx,
            dense_gk,
            acc_gate + dot_rows(part_x, gate_rows),
            acc_up + dot_rows(part_x, up_rows),
            acc_down + dot_rows(hidden, scaled),
        )

    initial = (
        jnp.zeros((slot_count, row_width), jnp.bfloat16),
        jnp.zeros((slot_count,), jnp.float32),
        jnp.zeros(gate_weight.shape, jnp.float32),
        jnp.zeros(up_weight.shape, jnp.float32),
        jnp.zeros(down_weight.shape, jnp.float32),
    )
    dense_dx, dense_gk, acc_gate, acc_up, acc_down = lax.fori_loop(0, nblocks, block_step, initial)
    inverse = (starts[:, None] + jnp.arange(capacity, dtype=jnp.int32)[None, :]).reshape(slot_count)
    inverse = jnp.where(live_mask.reshape(slot_count), inverse, 0)
    flat_live = live_mask.reshape(slot_count)
    dx_slots = jnp.where(flat_live[:, None], dense_dx[inverse], jnp.zeros((), jnp.bfloat16))
    gk_slots = jnp.where(flat_live, dense_gk[inverse], jnp.zeros((), jnp.float32)).astype(
        jnp.bfloat16
    )
    return (
        dx_slots.reshape(sources, capacity, row_width),
        gk_slots.reshape(sources, capacity),
        (acc_gate, acc_up, acc_down),
    )


def shards(tokens, grad_out, combine, expert_ids, w_gate, w_up, w_down):
    tok_dev, top_count = expert_ids.shape
    owners = lax.axis_size("ep")
    capacity = tok_dev // 2
    slot_count = owners * capacity
    entries = tok_dev * top_count
    flat_ids = expert_ids.reshape(entries)
    flat_w = combine.reshape(entries)
    experts_iota = jnp.arange(owners, dtype=jnp.int32)
    member = (flat_ids[:, None] == experts_iota[None, :]).astype(jnp.int32)
    rank_in = jnp.sum(jnp.cumsum(member, axis=0) * member, axis=1) - 1
    slot_iota = jnp.arange(slot_count, dtype=jnp.int32)
    slot_expert = slot_iota // capacity
    slot_rank = slot_iota % capacity
    matches = (flat_ids[None, :] == slot_expert[:, None]) & (rank_in[None, :] == slot_rank[:, None])
    select = jnp.any(matches.reshape(slot_count, tok_dev, top_count), axis=2).astype(jnp.bfloat16)
    send_x = dot_plain(select, tokens).astype(jnp.bfloat16).reshape(owners, capacity, -1)
    send_dy = dot_plain(select, grad_out).astype(jnp.bfloat16).reshape(owners, capacity, -1)
    send_w = jnp.sum(jnp.where(matches, flat_w[None, :].astype(jnp.float32), 0.0), axis=1)
    send_w = send_w.astype(jnp.bfloat16).reshape(owners, capacity)
    gate_local = w_gate[0]
    up_local = w_up[0]
    down_local = w_down[0]
    received = (
        lax.all_to_all(send_x, "ep", split_axis=0, concat_axis=0, tiled=True),
        lax.all_to_all(send_dy, "ep", split_axis=0, concat_axis=0, tiled=True),
        lax.all_to_all(send_w, "ep", split_axis=0, concat_axis=0, tiled=True),
    )
    dx_slots, gk_slots, partials = owner_blocks(
        received[0], received[1], received[2], gate_local, up_local, down_local
    )
    back_dx, back_gk = (
        lax.all_to_all(dx_slots, "ep", split_axis=0, concat_axis=0, tiled=True),
        lax.all_to_all(gk_slots, "ep", split_axis=0, concat_axis=0, tiled=True),
    )
    grad_tokens = dot_rows(select, back_dx.reshape(slot_count, -1)).astype(jnp.bfloat16)
    grad_combine = jnp.dot(
        back_gk.reshape(slot_count),
        matches.astype(jnp.bfloat16),
        preferred_element_type=jnp.float32,
    )
    grad_combine = grad_combine.reshape(tok_dev, top_count).astype(jnp.bfloat16)
    acc_gate, acc_up, acc_down = partials
    sum_gate, sum_up, sum_down = (
        lax.psum_scatter(
            acc_gate[None].astype(jnp.bfloat16), "grp", scatter_dimension=1, tiled=True
        ).astype(jnp.float32),
        lax.psum_scatter(
            acc_up[None].astype(jnp.bfloat16), "grp", scatter_dimension=1, tiled=True
        ).astype(jnp.float32),
        lax.psum_scatter(
            acc_down[None].astype(jnp.bfloat16), "grp", scatter_dimension=2, tiled=True
        ).astype(jnp.float32),
    )
    return (
        grad_tokens,
        grad_combine,
        sum_gate.astype(jnp.bfloat16),
        sum_up.astype(jnp.bfloat16),
        sum_down.astype(jnp.bfloat16),
    )


def solution(mesh):
    placed = (
        P(("grp", "ep"), None),
        P(("grp", "ep"), None),
        P(("grp", "ep"), None),
        P(("grp", "ep"), None),
        P("ep", None, None),
        P("ep", None, None),
        P("ep", None, None),
    )
    return jax.shard_map(
        shards,
        mesh=mesh,
        in_specs=placed,
        out_specs=(
            P(("grp", "ep"), None),
            P(("grp", "ep"), None),
            P("ep", "grp", None),
            P("ep", "grp", None),
            P("ep", None, "grp"),
        ),
        check_vma=False,
    )
```

profile of v0, /device:TPU:32, one launch (start us, length us, event | category | flops | bytes accessed | tf_op | source)
XLA Modules:
  0.0 566.2 jit_solution(12170161169397140330)
XLA Ops:
  11.4 11.6 %all-to-all-start = ((bf16[64,1,16]{2,1,0:T(2,128)(2,1)}), bf16[64,1,16]{2,1,0:T(2,128)(2,1)S(1)}, u32[]{:S(2)}, u32[]{:S(2)}) async-start(bf16[64,1,16]{2,1,0:T(2,128)(2,1)} %convert_element_type.116), calls=%async_computation | async-start | bytes 65536 | tf_op jit(solution)/shard_map/all_to_all | solution.py:141
  24.3 3.3 convolution_convert_fusion.1
  27.5 3.9 all-to-all-done
  31.4 6.7 %all-to-all-start.1 = ((bf16[64,16,2048]{2,1,0:T(8,128)(2,1)}), bf16[64,16,2048]{2,1,0:T(8,128)(2,1)}, u32[]{:S(2)}, u32[]{:S(2)}) async-start(bf16[64,16,2048]{2,1,0:T(8,128)(2,1)} %bitcast.89), calls=%async_computation.1 | async-start | bytes 8388608 | tf_op jit(solution)/shard_map/all_to_all | solution.py:140
  38.2 3.3 convolution_convert_fusion
  41.5 90.8 %all-to-all-done.1 = bf16[64,16,2048]{2,1,0:T(8,128)(2,1)} async-done(((bf16[64,16,2048]{2,1,0:T(8,128)(2,1)}), bf16[64,16,2048]{2,1,0:T(8,128)(2,1)}, u32[]{:S(2)}, u32[]{:S(2)}) %all-to-all-start.1) | async-done | bytes 4194336 | tf_op jit(solution)/shard_map/all_to_all | solution.py:140
  132.3 7.7 %all-to-all-start.2 = ((bf16[64,16,2048]{2,1,0:T(8,128)(2,1)}), bf16[64,16,2048]{2,1,0:T(8,128)(2,1)}, u32[]{:S(2)}, u32[]{:S(2)}) async-start(bf16[64,16,2048]{2,1,0:T(8,128)(2,1)} %bitcast.88), calls=%async_computation.2 | async-start | bytes 8388608 | tf_op jit(solution)/shard_map/all_to_all | solution.py:139
  143.0 6.8 %gather_fusion = bf16[1024]{0:T(1024)(128)(2,1)S(1)} fusion(bf16[1024]{0:T(1024)(128)(2,1)S(1)} %reshape.287, s32[1024]{0:T(1024)S(1)} %broadcast_clamp_fusion.1), kind=kCustom, calls=%fused_computation | custom fusion | bytes 8192 | tf_op jit(solution)/shard_map/gather | solution.py:70
  151.1 11.6 %gather_fusion.1 = bf16[1024,2048]{1,0:T(8,128)(2,1)} fusion(bf16[1024,2048]{1,0:T(8,128)(2,1)} %bitcast.7, s32[1024]{0:T(1024)S(1)} %broadcast_clamp_fusion.1), kind=kCustom, calls=%fused_computation.1 | custom fusion | bytes 8392704 | tf_op jit(solution)/shard_map/gather | solution.py:67
  162.7 71.4 %all-to-all-done.2 = bf16[64,16,2048]{2,1,0:T(8,128)(2,1)} async-done(((bf16[64,16,2048]{2,1,0:T(8,128)(2,1)}), bf16[64,16,2048]{2,1,0:T(8,128)(2,1)}, u32[]{:S(2)}, u32[]{:S(2)}) %all-to-all-start.2) | async-done | bytes 4194336 | tf_op jit(solution)/shard_map/all_to_all | solution.py:139
  234.1 11.6 %gather_fusion.2 = bf16[1024,2048]{1,0:T(8,128)(2,1)} fusion(bf16[1024,2048]{1,0:T(8,128)(2,1)} %bitcast.10, s32[1024]{0:T(1024)S(1)} %broadcast_clamp_fusion.1), kind=kCustom, calls=%fused_computation.2 | custom fusion | bytes 8392704 | tf_op jit(solution)/shard_map/gather | solution.py:62
  245.7 5.9 %broadcast_select_fusion = (bf16[1024,2048]{1,0:T(8,128)(2,1)}, bf16[1024,2048]{1,0:T(8,128)(2,1)}) fusion(bf16[1024,2048]{1,0:T(8,128)(2,1)} %gather_fusion.2, pred[1024]{0:T(1024)(128)(4,1)S(1)} %iota_compare_fusion.3, bf16[1024,2048]{1,0:T(8,128)(2,1)} %gather_fusion.1), kind=kLoop, calls=%fused_computation.34 | loop fusion | flops 4194304 | bytes 16778240 | tf_op jit(solution)/shard_map/jit(_where)/select_n | solution.py:60
  251.6 2.5 broadcast.235
  254.1 2.5 broadcast.235.clone
  256.6 2.4 broadcast_in_dim.77
  259.0 2.5 broadcast_in_dim.79
  261.5 38.7 %while.18 = (s32[]{:T(128)}, bf16[1024,2048]{1,0:T(8,128)(2,1)}, bf16[1024]{0:T(1024)(128)(2,1)S(1)}, f32[2048,512]{1,0:T(8,128)}, f32[2048,512]{1,0:T(8,128)}, ...) while((s32[]{:T(128)}, bf16[1024,2048]{1,0:T(8,128)(2,1)}, ...), condition=%wide.region_12.13_spmd, body=%wide.region_10.12_spmd.sunk | while | flops 2422931456 | bytes 163711952 | solution.py:100
  263.6 2.2 fusion.89
  276.3 2.2 convolution_add_fusion.8
  282.9 2.2 fusion.89
  295.5 2.2 convolution_add_fusion.8
  300.2 3.8 convert_bitcast_fusion.2
  304.6 11.6 %gather_fusion.3 = bf16[1024,2048]{1,0:T(8,128)(2,1)} fusion(bf16[1024,2048]{1,0:T(8,128)(2,1)} %get-tuple-element.77, s32[1024]{0:T(1024)S(1)} %broadcast_clamp_fusion), kind=kCustom, calls=%fused_computation.3 | custom fusion | bytes 8392704 | tf_op jit(solution)/shard_map/gather | solution.py:104
  316.1 6.8 %gather_fusion.4 = bf16[1024]{0:T(1024)(128)(2,1)S(1)} fusion(bf16[1024]{0:T(1024)(128)(2,1)S(1)} %get-tuple-element.78, s32[1024]{0:T(1024)S(1)} %broadcast_clamp_fusion), kind=kCustom, calls=%fused_computation.4 | custom fusion | bytes 8192 | tf_op jit(solution)/shard_map/gather | solution.py:105
  323.8 123.0 %all-to-all-start.4 = ((bf16[64,1,16]{2,1,0:T(2,128)(2,1)}), bf16[64,1,16]{2,1,0:T(2,128)(2,1)S(1)}, u32[]{:S(2)}, u32[]{:S(2)}) async-start(bf16[64,1,16]{2,1,0:T(2,128)(2,1)} %copy.53), calls=%async_computation.4 | async-start | bytes 65536 | tf_op jit(solution)/shard_map/all_to_all | solution.py:148
  446.8 4.5 broadcast_select_fusion.2
  451.4 4.0 all-to-all-done.4
  455.3 6.6 %all-to-all-start.3 = ((bf16[64,16,2048]{2,1,0:T(8,128)(2,1)}), bf16[64,16,2048]{2,1,0:T(8,128)(2,1)}, u32[]{:S(2)}, u32[]{:S(2)}) async-start(bf16[64,16,2048]{2,1,0:T(8,128)(2,1)} %broadcast_select_fusion.2), calls=%async_computation.3 | async-start | bytes 8388608 | tf_op jit(solution)/shard_map/all_to_all | solution.py:147
  461.9 3.8 convert_bitcast_fusion.1
  465.8 3.9 convert_bitcast_fusion
  471.7 84.2 %all-to-all-done.3 = bf16[64,16,2048]{2,1,0:T(8,128)(2,1)} async-done(((bf16[64,16,2048]{2,1,0:T(8,128)(2,1)}), bf16[64,16,2048]{2,1,0:T(8,128)(2,1)}, u32[]{:S(2)}, u32[]{:S(2)}) %all-to-all-start.3) | async-done | bytes 4194336 | tf_op jit(solution)/shard_map/all_to_all | solution.py:147
  556.0 3.6 convolution_convert_fusion.2
  (116 shorter events, 41.9 us)
Async XLA Ops:
  7.2 17.1 %copy-start = (bf16[32,2048]{1,0:T(8,128)(2,1)S(1)}, bf16[32,2048]{1,0:T(8,128)(2,1)}, u32[]{:S(2)}) copy-start(bf16[32,2048]{1,0:T(8,128)(2,1)} %param.10) | copy-start | bytes 393220
  11.4 20.1 %all-to-all-start = ((bf16[64,1,16]{2,1,0:T(2,128)(2,1)}), bf16[64,1,16]{2,1,0:T(2,128)(2,1)S(1)}, u32[]{:S(2)}, u32[]{:S(2)}) async-start(bf16[64,1,16]{2,1,0:T(2,128)(2,1)} %convert_element_type.116), calls=%async_computation | async-start | bytes 65536 | tf_op jit(solution)/shard_map/all_to_all | solution.py:141
  31.4 6.8 %copy-start.11 = (bf16[32,2048]{1,0:T(8,128)(2,1)S(1)}, bf16[32,2048]{1,0:T(8,128)(2,1)}, u32[]{:S(2)}) copy-start(bf16[32,2048]{1,0:T(8,128)(2,1)} %param.9) | copy-start | bytes 393220
  31.4 100.8 %all-to-all-start.1 = ((bf16[64,16,2048]{2,1,0:T(8,128)(2,1)}), bf16[64,16,2048]{2,1,0:T(8,128)(2,1)}, u32[]{:S(2)}, u32[]{:S(2)}) async-start(bf16[64,16,2048]{2,1,0:T(8,128)(2,1)} %bitcast.89), calls=%async_computation.1 | async-start | bytes 8388608 | tf_op jit(solution)/shard_map/all_to_all | solution.py:140
  132.3 101.8 %all-to-all-start.2 = ((bf16[64,16,2048]{2,1,0:T(8,128)(2,1)}), bf16[64,16,2048]{2,1,0:T(8,128)(2,1)}, u32[]{:S(2)}, u32[]{:S(2)}) async-start(bf16[64,16,2048]{2,1,0:T(8,128)(2,1)} %bitcast.88), calls=%async_computation.2 | async-start | bytes 8388608 | tf_op jit(solution)/shard_map/all_to_all | solution.py:139
  140.0 419.6 %reduce-scatter.4.cloned.1.call-start = ((), (), s32[]{:S(2)}) async-start(), calls=%async_computation.8 | async-start | bytes 2621440 | tf_op jit(solution)/shard_map/reduce_scatter | solution.py:159
  256.6 4.9 copy-start.2
  261.5 4.3 copy-start.10
  261.6 5.8 %copy-start.3 = (bf16[2048,512]{1,0:T(8,128)(2,1)S(1)}, bf16[2048,512]{1,0:T(8,128)(2,1)}, u32[]{:S(2)}) copy-start(bf16[2048,512]{1,0:T(8,128)(2,1)} %get-tuple-element.252) | copy-start | bytes 6291460 | tf_op jit(solution)/shard_map/while
  267.4 2.5 copy-start.8
  269.9 4.0 copy-start.4
  272.0 2.0 copy-start.9
  273.9 2.3 copy-start.6
  275.9 2.6 copy-start.5
  278.5 2.0 copy-start.7
  280.8 4.3 copy-start.10
  280.8 5.8 %copy-start.3 = (bf16[2048,512]{1,0:T(8,128)(2,1)S(1)}, bf16[2048,512]{1,0:T(8,128)(2,1)}, u32[]{:S(2)}) copy-start(bf16[2048,512]{1,0:T(8,128)(2,1)} %get-tuple-element.252) | copy-start | bytes 6291460 | tf_op jit(solution)/shard_map/while
  286.7 2.5 copy-start.8
  289.2 4.0 copy-start.4
  291.2 2.0 copy-start.9
  293.2 2.3 copy-start.6
  295.2 2.6 copy-start.5
  297.8 2.0 copy-start.7
  323.8 131.5 %all-to-all-start.4 = ((bf16[64,1,16]{2,1,0:T(2,128)(2,1)}), bf16[64,1,16]{2,1,0:T(2,128)(2,1)S(1)}, u32[]{:S(2)}, u32[]{:S(2)}) async-start(bf16[64,1,16]{2,1,0:T(2,128)(2,1)} %copy.53), calls=%async_computation.4 | async-start | bytes 65536 | tf_op jit(solution)/shard_map/all_to_all | solution.py:148
  455.3 100.6 %all-to-all-start.3 = ((bf16[64,16,2048]{2,1,0:T(8,128)(2,1)}), bf16[64,16,2048]{2,1,0:T(8,128)(2,1)}, u32[]{:S(2)}, u32[]{:S(2)}) async-start(bf16[64,16,2048]{2,1,0:T(8,128)(2,1)} %broadcast_select_fusion.2), calls=%async_computation.3 | async-start | bytes 8388608 | tf_op jit(solution)/shard_map/all_to_all | solution.py:147
  461.9 97.7 %reduce-scatter.6.cloned.1.call-start = ((), (), s32[]{:S(2)}) async-start(), calls=%async_computation.9 | async-start | bytes 2621440 | tf_op jit(solution)/shard_map/reduce_scatter | solution.py:162
  465.7 93.9 %reduce-scatter.8.cloned.1.call-start = ((), (), s32[]{:S(2)}) async-start(), calls=%async_computation.10 | async-start | bytes 2621440 | tf_op jit(solution)/shard_map/reduce_scatter | solution.py:165
  469.7 90.0 %copy-start.1 = (bf16[32,2048]{1,0:T(8,128)(2,1)S(1)}, bf16[32,2048]{1,0:T(8,128)(2,1)}, u32[]{:S(2)}) copy-start(bf16[32,2048]{1,0:T(8,128)(2,1)} %param.10) | copy-start | bytes 393220
Sparse Core Ops, SparseCore 0:
  304.2 146.2 reduce-scatter.3
  466.0 33.5 reduce-scatter.5
  502.8 31.9 reduce-scatter.7
where the time goes:
time: 572 us; the launch traced here: 566 us
  waiting for transfers between devices  254 us (44%)
  starting transfers between devices  156 us (27%)
  local copies, waits for them, and re-layouts  68.6 us (12%)
  matrix products  43.8 us (8%)
  other arithmetic  28.3 us (5%)
  between operations  14.7 us (3%)
    all_to_all x1, starting transfers between devices, shards(): lax.all_to_all(gk_slots, 'ep', split_axis=0, concat_axis=0, tiled=True)  123 us
    all_to_all x1, waiting for transfers between devices, shards(): lax.all_to_all(send_dy, 'ep', split_axis=0, concat_axis=0, tiled=True)  90.8 us
    all_to_all x1, waiting for transfers between devices, shards(): lax.all_to_all(dx_slots, 'ep', split_axis=0, concat_axis=0, tiled=True)  84.2 us
    all_to_all x1, waiting for transfers between devices, shards(): lax.all_to_all(send_x, 'ep', split_axis=0, concat_axis=0, tiled=True)  71.4 us
    dot_general x8, matrix products, dot_plain(): return jnp.dot(left, right, preferred_element_type=jnp.float32)  18.1 us
    dot_general x7, matrix products, dot_rows(): lax.dot_general(left, right, (((0,), (0,)), ((), ())), preferred_element_...  16.3 us
    all_to_all x1, starting transfers between devices, shards(): lax.all_to_all(send_w, 'ep', split_axis=0, concat_axis=0, tiled=True)  11.6 us
    gather x1, local copies, waits for them, and re-layouts, owner_blocks(): recv_dy.reshape(slot_count, row_width)[pick_row]  11.6 us
  transfers between devices with their start and end apart: 8, of which 5 were waited for; matrix products, arithmetic and copies ran while one was open for 12% of the time, Pallas kernels for 0%

commit v1 on v0

v1 whole, which is shorter than its diff:
```python
import functools

import jax
import jax.numpy as jnp
from jax import lax
from jax.experimental import pallas as pl
from jax.experimental.pallas import tpu as pltpu
from jax.sharding import PartitionSpec as P

MESH = pl.DeviceIdType.MESH
F32 = jnp.float32
BF16 = jnp.bfloat16

NX, NZ, NG = 4, 8, 4
TOK = 32
HALF = TOK // 2
CAP = 16
LANES = 128
XO = (0, 1, -1, 2)
ZO = (0, 1, -1, 2, -2, 3, -3, 4)
BLOCKS = NX * NZ
CHUNK = 8
CTOK = CHUNK * TOK
CROW = CHUNK * CAP
ROUNDS = 2 * BLOCKS // CHUNK


def slot_of(kind, ox, oz):
    xi, zi = XO.index(ox), ZO.index(oz)
    return zi * NX + xi if kind == 0 else xi * NZ + zi


def dot(left, right, dims=((1,), (0,))):
    return lax.dot_general(left, right, (dims, ((), ())), preferred_element_type=F32)


def kernel(
    tokens,
    grad_out,
    combine,
    expert_ids,
    w_gate,
    w_up,
    w_down,
    o_tokens,
    o_combine,
    o_gate,
    o_up,
    o_down,
    buf,
    wg,
    wu,
    wd,
    rows_all,
    rows_t,
    pair,
    grads,
    sib,
    ysend,
    yrecv,
    xfar,
    xnear,
    znear,
    in_sem,
    ag_send,
    ag_recv,
    core_send,
    sib_send,
    sib_recv,
    y_send,
    y_recv,
    xf_send,
    xf_recv,
    xn_send,
    xn_recv,
    z_send,
    z_recv,
):
    width = tokens.shape[1]
    hidden_width = w_gate.shape[1]
    part = width // NG
    fhalf = hidden_width // 2
    grad_width = width + LANES
    me = lax.axis_index("ep")
    group = lax.axis_index("grp")
    core = me % 2
    zpos = (me // 2) % NZ
    xpos = me // (2 * NZ)

    def at(dx, dz):
        return {"ep": (((xpos + dx + NX) % NX) * NZ + (zpos + dz + NZ) % NZ) * 2 + core}

    sibling = {"ep": me + 1 - 2 * core}
    y_next = {"grp": (group + 1) % NG}
    y_prev = {"grp": (group + NG - 1) % NG}
    x_next, x_prev, z_next, z_prev = at(1, 0), at(-1, 0), at(0, 1), at(0, -1)

    barrier = pltpu.get_barrier_semaphore()
    for other in (sibling, x_next, x_prev, z_next, z_prev, y_next, y_prev):
        pl.semaphore_signal(barrier, inc=1, device_id=other, device_id_type=MESH)

    loads = [
        pltpu.make_async_copy(tokens, buf.at[core, pl.ds(0, TOK), pl.ds(0, width)], in_sem.at[0]),
        pltpu.make_async_copy(
            grad_out, buf.at[core, pl.ds(0, TOK), pl.ds(width, width)], in_sem.at[1]
        ),
        pltpu.make_async_copy(w_gate, wg, in_sem.at[2]),
        pltpu.make_async_copy(w_up, wu, in_sem.at[3]),
        pltpu.make_async_copy(w_down, wd, in_sem.at[4]),
    ]
    for load in loads:
        load.start()
    lane_iota = lax.broadcasted_iota(jnp.int32, (TOK, LANES), 1)
    ids = expert_ids[...]
    weights = combine[...].astype(F32)
    table = jnp.zeros((TOK, LANES), F32)
    for k in range(ids.shape[1]):
        table = table + jnp.where(ids[:, k : k + 1] == lane_iota, weights[:, k : k + 1], 0.0)
    buf[core, 0:TOK, 2 * width : 2 * width + LANES] = table.astype(BF16)
    loads[0].wait()
    loads[1].wait()
    pl.semaphore_wait(barrier, 7)

    hops, shares = ({}, {}), ({}, {})

    def span(slot, half):
        if half is None:
            return pl.ds(slot * TOK, TOK)
        return pl.ds(slot * TOK + half * HALF, HALF)

    def hop(kind, source, target, other, half=None):
        a, b = slot_of(kind, *source), slot_of(kind, *target)
        index = (kind * BLOCKS + b) * 2 + (half or 0)
        return pltpu.make_async_remote_copy(
            src_ref=buf.at[kind, span(a, half)],
            dst_ref=buf.at[kind, span(b, half)],
            send_sem=ag_send.at[index],
            recv_sem=ag_recv.at[index],
            device_id=other,
            device_id_type=MESH,
        )

    def send(kind, source, target, other, half=None):
        hop(kind, source, target, other, half).start()
        hops[kind][target, half] = source, other

    def across(kind, slot):
        return pltpu.make_async_remote_copy(
            src_ref=buf.at[kind, span(slot, None)],
            dst_ref=buf.at[kind, span(slot, None)],
            send_sem=core_send.at[slot],
            recv_sem=ag_recv.at[(kind * BLOCKS + slot) * 2],
            device_id=sibling,
            device_id_type=MESH,
        )

    def share(kind, offset):
        across(kind, slot_of(kind, *offset)).start()
        shares[kind][offset] = True

    def arrive(kind, offset, half=None):
        hop(kind, offset, offset, z_next, half).wait_recv()

    def z_out(kind, ox, oz):
        if oz == 0:
            send(kind, (ox, 0), (ox, 1), z_next)
            send(kind, (ox, 0), (ox, -1), z_prev)
        elif oz == 3:
            send(kind, (ox, 3), (ox, 4), z_next, half=0)
        elif oz == -3:
            send(kind, (ox, -3), (ox, 4), z_prev, half=1)
        elif oz > 0:
            send(kind, (ox, oz), (ox, oz + 1), z_next)
        else:
            send(kind, (ox, oz), (ox, oz - 1), z_prev)

    def x_out(oz):
        send(1, (0, oz), (1, oz), x_next)
        send(1, (0, oz), (-1, oz), x_prev)

    def first_round(kind):
        if kind == 0:
            send(0, (0, 0), (1, 0), x_next)
            send(0, (0, 0), (-1, 0), x_prev)
            z_out(0, 0, 0)
            share(0, (0, 0))
            arrive(0, (1, 0))
            send(0, (1, 0), (2, 0), x_next, half=0)
            z_out(0, 1, 0)
            share(0, (1, 0))
            arrive(0, (-1, 0))
            send(0, (-1, 0), (2, 0), x_prev, half=1)
            z_out(0, -1, 0)
            share(0, (-1, 0))
            arrive(0, (2, 0), 0)
            arrive(0, (2, 0), 1)
            z_out(0, 2, 0)
            share(0, (2, 0))
            z_round(1)
        else:
            z_out(1, 0, 0)
            x_out(0)
            share(1, (0, 0))
            for oz in (1, -1, 2, -2):
                arrive(1, (0, oz))
                z_out(1, 0, oz)
                x_out(oz)
                share(1, (0, oz))

    def z_round(k):
        for ox in XO:
            for oz in (k, -k):
                arrive(0, (ox, oz))
                z_out(0, ox, oz)
                share(0, (ox, oz))

    def z_last():
        for ox in XO:
            arrive(0, (ox, 4), 0)
            arrive(0, (ox, 4), 1)
            share(0, (ox, 4))

    def x_near(offsets):
        for oz in offsets:
            even = ZO.index(oz) % 2 == 0
            arrive(1, (1, oz))
            if even:
                send(1, (1, oz), (2, oz), x_next)
            share(1, (1, oz))
            arrive(1, (-1, oz))
            if not even:
                send(1, (-1, oz), (2, oz), x_prev)
            share(1, (-1, oz))

    def x_far(offsets):
        for oz in offsets:
            arrive(1, (2, oz))
            share(1, (2, oz))

    def second_round():
        for oz in (3, -3):
            arrive(1, (0, oz))
            z_out(1, 0, oz)
            x_out(oz)
            share(1, (0, oz))
        x_near((0,))
        arrive(1, (0, 4), 0)
        arrive(1, (0, 4), 1)
        x_out(4)
        share(1, (0, 4))

    plans = (
        {
            0: lambda: first_round(0),
            2: lambda: z_round(2),
            4: lambda: z_round(3),
            6: z_last,
        },
        {
            0: lambda: first_round(1),
            1: second_round,
            2: lambda: x_near((1, -1, 2, -2)),
            3: lambda: x_near((3, -3, 4)),
            5: lambda: x_far((0, 1, -1)),
            6: lambda: x_far((2, -2)),
            7: lambda: x_far((3, -3, 4)),
        },
    )

    def pair_copy(kind, rows):
        return pltpu.make_async_remote_copy(
            src_ref=grads.at[kind, rows],
            dst_ref=sib.at[rows],
            send_sem=sib_send.at[rows.start // CTOK],
            recv_sem=sib_recv.at[rows.start // CTOK],
            device_id=sibling,
            device_id_type=MESH,
        )

    def chunk(step, kind):
        first = pl.multiple_of((step // 2) * CTOK, CTOK)
        rows = pl.ds(first, CTOK)
        packed = pl.ds(pl.multiple_of(step * CROW, CROW), CROW)
        pick = (lax.broadcasted_iota(jnp.int32, (CAP, LANES), 1) == me).astype(F32).astype(BF16)
        table = buf[kind, rows, 2 * width : 2 * width + LANES]
        weight_row = dot(pick, table, ((1,), (1,)))
        routed = jnp.where(weight_row > 0, 1.0, 0.0)
        row_id = lax.broadcasted_iota(jnp.int32, (CTOK, CTOK), 0)
        col_id = lax.broadcasted_iota(jnp.int32, (CTOK, CTOK), 1)
        upto = (row_id <= col_id) & (row_id // TOK == col_id // TOK)
        rank = dot(routed.astype(BF16), upto.astype(F32).astype(BF16))
        base = (lax.broadcasted_iota(jnp.int32, (1, CTOK), 1) // TOK * CAP).astype(F32)
        target = jnp.where(routed[0:1] > 0, base + rank[0:1] - 1.0, -1.0)
        place = lax.broadcasted_iota(jnp.int32, (CROW, CTOK), 0).astype(F32)
        select = jnp.where(place == target, 1.0, 0.0)
        weight = jnp.sum(select * weight_row[0:1], axis=1, keepdims=True)
        select_t = select.T.astype(BF16)
        select = select.astype(BF16)
        for c in range(2 * NG):
            cols = slice((c % NG) * part, (c % NG + 1) * part)
            picked = dot(select, buf[kind, rows, c * part : (c + 1) * part])
            rows_all[c // NG, packed, cols] = picked.astype(BF16)

        combine_grad = jnp.zeros((CROW, 1), F32)
        for f in range(2):
            cols = slice(f * fhalf, (f + 1) * fhalf)
            x_rows = rows_all[0, packed, :]
            pre_gate = dot(x_rows, wg[:, cols])
            pre_up = dot(x_rows, wu[:, cols])
            back = dot(rows_all[1, packed, :], wd[cols, :], ((1,), (1,)))
            sigmoid = jax.nn.sigmoid(pre_gate)
            activation = pre_gate * sigmoid
            derivative = sigmoid * (1.0 + pre_gate * (1.0 - sigmoid))
            hidden = activation * pre_up
            combine_grad = combine_grad + jnp.sum(hidden * back, axis=1, keepdims=True)
            back = back * weight
            gate_rows = back * pre_up * derivative
            up_rows = back * activation
            pair[0, :, cols] = gate_rows.astype(BF16)
            pair[1, :, cols] = up_rows.astype(BF16)
            rows_t[0, cols, packed] = gate_rows.T.astype(BF16)
            rows_t[1, cols, packed] = up_rows.T.astype(BF16)
            rows_t[2, cols, packed] = (hidden * weight).T.astype(BF16)

        for c in range(NG):
            cols = slice(c * part, (c + 1) * part)
            row_grad = dot(pair[0], wg[cols, :], ((1,), (1,)))
            row_grad = row_grad + dot(pair[1], wu[cols, :], ((1,), (1,)))
            grads[kind, rows, cols] = dot(select_t, row_grad.astype(BF16)).astype(BF16)
        lanes = lax.broadcasted_iota(jnp.int32, (CROW, LANES), 1)
        spread = jnp.where(lanes == me, combine_grad, 0.0).astype(BF16)
        grads[kind, rows, width:grad_width] = dot(select_t, spread).astype(BF16)
        return rows

    def round_body(step, carry):
        kind = step % 2
        for c in range(2):
            for r, plan in plans[c].items():
                pl.when((step == r) & (core == c))(plan)

        @pl.when(kind != core)
        def _():
            def wait_block(i, carry):
                slot = (step // 2) * CHUNK + i
                pltpu.make_async_remote_copy(
                    src_ref=buf.at[kind, pl.ds(pl.multiple_of(slot * TOK, TOK), TOK)],
                    dst_ref=buf.at[kind, pl.ds(pl.multiple_of(slot * TOK, TOK), TOK)],
                    send_sem=core_send.at[slot],
                    recv_sem=ag_recv.at[(kind * BLOCKS + slot) * 2],
                    device_id=sibling,
                    device_id_type=MESH,
                ).wait_recv()
                return carry

            lax.fori_loop(0, CHUNK, wait_block, 0)

        @pl.when(step == 0)
        def _():
            for load in loads[2:]:
                load.wait()

        rows = chunk(step, kind)

        @pl.when(kind != core)
        def _():
            pair_copy(kind, rows).start()

        return carry

    lax.fori_loop(0, ROUNDS, round_body, 0)

    def tile(index, mat, half):
        left = rows_t[mat, half * fhalf : (half + 1) * fhalf, :]
        cols = pl.ds(pl.multiple_of(index * part, part), part)
        return dot(left, rows_all[0 if mat < 2 else 1, :, cols])

    def y_copy(source, step, way, mat):
        index = (step * 2 + way) * 3 + mat
        return pltpu.make_async_remote_copy(
            src_ref=source,
            dst_ref=yrecv.at[index],
            send_sem=y_send.at[index],
            recv_sem=y_recv.at[index],
            device_id=y_next if way == 0 else y_prev,
            device_id_type=MESH,
        )

    y_sent = []

    def y_task(step, mat):
        for way in range(2):
            shift = NG - 1 - step if way == 0 else 1 + step
            term = tile((group + shift) % NG, mat, way)
            if step == 0:
                source = ysend.at[way * 3 + mat]
                source[...] = term.astype(BF16)
            else:
                source = yrecv.at[((step - 1) * 2 + way) * 3 + mat]
                y_copy(source, step - 1, way, mat).wait_recv()
                term = term + source[...].astype(F32)
                if step < NG - 1:
                    source[...] = term.astype(BF16)
            if step < NG - 1:
                copy = y_copy(source, step, way, mat)
                copy.start()
                y_sent.append(copy)
            else:
                cols = slice(way * fhalf, (way + 1) * fhalf)
                if mat == 0:
                    o_gate[:, cols] = term.T.astype(BF16)
                elif mat == 1:
                    o_up[:, cols] = term.T.astype(BF16)
                else:
                    o_down[cols, :] = term.astype(BF16)

    def rows_of(ox, oz):
        a, b = slot_of(0, ox, oz), slot_of(1, ox, oz)
        return pl.multiple_of((a + (b - a) * core) * TOK, TOK)

    def block(ox, oz, half=None):
        first = rows_of(ox, oz)
        if half is None:
            return grads.at[core, pl.ds(first, TOK)]
        return grads.at[core, pl.ds(pl.multiple_of(first + half * HALF, HALF), HALF)]

    def push(source, target, send_sem, recv_sem, other):
        return pltpu.make_async_remote_copy(
            src_ref=source,
            dst_ref=target,
            send_sem=send_sem,
            recv_sem=recv_sem,
            device_id=other,
            device_id_type=MESH,
        )

    def far_copy(zi):
        oz = ZO[zi]
        other = x_prev if zi % 2 == 0 else x_next
        return push(block(2, oz), xfar.at[zi], xf_send.at[zi], xf_recv.at[zi], other)

    def near_copy(side, zi):
        oz = ZO[zi]
        index = side * NZ + zi
        other = x_prev if side == 0 else x_next
        return push(
            block(1 - 2 * side, oz), xnear.at[index], xn_send.at[index], xn_recv.at[index], other
        )

    def z_copy(side, k):
        sign = 1 - 2 * side
        other = z_prev if side == 0 else z_next
        index = side * 4 + k - 1
        target = znear.at[index]
        half = None
        if k == 4:
            half = side
            target = znear.at[index, pl.ds(side * HALF, HALF)]
        oz = 4 if k == 4 else sign * k
        return push(block(0, oz, half), target, z_send.at[index], z_recv.at[index], other)

    rs_sent = []

    def go(copy):
        copy.start()
        rs_sent.append(copy)

    def pair_sums():
        def body(i, carry):
            rows = pl.ds(pl.multiple_of(i * CTOK, CTOK), CTOK)
            copy = pair_copy(core, rows)
            copy.wait_recv()

            def piece(j, inner):
                part_rows = pl.ds(pl.multiple_of(i * CTOK + j * TOK, TOK), TOK)
                total = grads[core, part_rows, :].astype(F32) + sib[part_rows, :].astype(F32)
                grads[core, part_rows, :] = total.astype(BF16)
                return inner

            return lax.fori_loop(0, CHUNK, piece, carry)

        lax.fori_loop(0, BLOCKS // CHUNK, body, 0)

    zi_order = (7, 5, 6, 3, 4, 1, 2, 0)

    def x_start():
        for zi in zi_order:
            go(far_copy(zi))
        for zi in zi_order:
            go(near_copy(1 if zi % 2 == 0 else 0, zi))

    def x_add(zis):
        for zi in zis:
            side = 0 if zi % 2 == 0 else 1
            far_copy(zi).wait_recv()
            mine = block(1 - 2 * side, ZO[zi])
            mine[...] = (mine[...].astype(F32) + xfar[zi].astype(F32)).astype(BF16)
            go(near_copy(side, zi))

    def x_total(oz):
        zi = ZO.index(oz)
        near_copy(0, zi).wait_recv()
        near_copy(1, zi).wait_recv()
        mine = block(0, oz)
        return mine[...].astype(F32) + xnear[zi].astype(F32) + xnear[NZ + zi].astype(F32)

    def z_task(oz):
        total = x_total(oz)
        if oz == 4:
            block(0, oz)[...] = total.astype(BF16)
            go(z_copy(0, 4))
            go(z_copy(1, 4))
            return
        side = 0 if oz > 0 else 1
        k = abs(oz)
        index = side * 4 + k
        z_copy(side, k + 1).wait_recv()
        if k == 3:
            block(0, oz)[...] = total.astype(BF16)
            mine = block(0, oz, side)
            got = znear[index, side * HALF : (side + 1) * HALF, :]
            mine[...] = (mine[...].astype(F32) + got.astype(F32)).astype(BF16)
        else:
            block(0, oz)[...] = (total + znear[index].astype(F32)).astype(BF16)
        go(z_copy(side, k))

    def z_final():
        total = x_total(0)
        z_copy(0, 1).wait_recv()
        z_copy(1, 1).wait_recv()
        total = total + znear[0].astype(F32) + znear[4].astype(F32)
        o_tokens[...] = total[:, :width].astype(BF16)
        by_expert = total[:, width:grad_width]
        column = lax.broadcasted_iota(jnp.int32, o_combine.shape, 1)
        out = jnp.zeros(o_combine.shape, F32)
        for k in range(o_combine.shape[1]):
            value = jnp.sum(
                jnp.where(expert_ids[:, k : k + 1] == lane_iota, by_expert, 0.0),
                axis=1,
                keepdims=True,
            )
            out = out + jnp.where(column == k, value, 0.0)
        o_combine[...] = out.astype(BF16)

    for mat in range(3):
        y_task(0, mat)
    pair_sums()
    x_start()
    y_task(1, 0)
    y_task(1, 1)
    x_add(zi_order[:4])
    y_task(1, 2)
    x_add(zi_order[4:])
    y_task(2, 0)
    y_task(2, 1)
    z_task(4)
    z_task(3)
    z_task(-3)
    y_task(2, 2)
    z_task(2)
    z_task(-2)
    z_task(1)
    z_task(-1)
    y_task(3, 0)
    z_final()
    y_task(3, 1)
    y_task(3, 2)

    for kind in range(2):

        @pl.when(core == kind)
        def _(kind=kind):
            for (target, half), (source, other) in hops[kind].items():
                hop(kind, source, target, other, half).wait_send()
            for offset in shares[kind]:
                across(kind, slot_of(kind, *offset)).wait_send()

    def pair_done(i, carry):
        pair_copy(1 - core, pl.ds(pl.multiple_of(i * CTOK, CTOK), CTOK)).wait_send()
        return carry

    lax.fori_loop(0, BLOCKS // CHUNK, pair_done, 0)
    for copy in y_sent + rs_sent:
        copy.wait_send()


def shards(tokens, grad_out, combine, expert_ids, w_gate, w_up, w_down):
    tok, width = tokens.shape
    top = expert_ids.shape[1]
    ff = w_gate.shape[2]
    part = width // NG
    slots = BLOCKS * TOK
    picked = ROUNDS * CROW
    gw = width + LANES
    any_spec = pl.BlockSpec(memory_space=pl.ANY)
    vmem_spec = pl.BlockSpec(memory_space=pltpu.VMEM)
    dma = pltpu.SemaphoreType.DMA
    results = pl.pallas_call(
        kernel,
        out_shape=(
            jax.ShapeDtypeStruct((tok, width), BF16),
            jax.ShapeDtypeStruct((tok, top), BF16),
            jax.ShapeDtypeStruct((part, ff), BF16),
            jax.ShapeDtypeStruct((part, ff), BF16),
            jax.ShapeDtypeStruct((ff, part), BF16),
        ),
        in_specs=[any_spec, any_spec, vmem_spec, vmem_spec, any_spec, any_spec, any_spec],
        out_specs=[vmem_spec] * 5,
        scratch_shapes=[
            pltpu.VMEM((2, slots, 2 * width + LANES), BF16),
            pltpu.VMEM((width, ff), BF16),
            pltpu.VMEM((width, ff), BF16),
            pltpu.VMEM((ff, width), BF16),
            pltpu.VMEM((2, picked, width), BF16),
            pltpu.VMEM((3, ff, picked), BF16),
            pltpu.VMEM((2, CROW, ff), BF16),
            pltpu.VMEM((2, slots, gw), BF16),
            pltpu.VMEM((slots, gw), BF16),
            pltpu.VMEM((6, ff // 2, part), BF16),
            pltpu.VMEM((18, ff // 2, part), BF16),
            pltpu.VMEM((NZ, tok, gw), BF16),
            pltpu.VMEM((2 * NZ, tok, gw), BF16),
            pltpu.VMEM((8, tok, gw), BF16),
            dma((5,)),
            dma((4 * BLOCKS,)),
            dma((4 * BLOCKS,)),
            dma((BLOCKS,)),
            dma((BLOCKS // CHUNK,)),
            dma((BLOCKS // CHUNK,)),
            dma((18,)),
            dma((18,)),
            dma((NZ,)),
            dma((NZ,)),
            dma((2 * NZ,)),
            dma((2 * NZ,)),
            dma((8,)),
            dma((8,)),
        ],
        compiler_params=pltpu.CompilerParams(
            collective_id=0, has_side_effects=True, vmem_limit_bytes=63 << 20
        ),
    )(tokens, grad_out, combine, expert_ids, w_gate[0], w_up[0], w_down[0])
    g_tokens, g_combine, g_gate, g_up, g_down = results
    return g_tokens, g_combine, g_gate[None], g_up[None], g_down[None]


def solution(mesh):
    rows = P(("grp", "ep"), None)
    expert = P("ep", None, None)
    return jax.shard_map(
        shards,
        mesh=mesh,
        in_specs=(rows, rows, rows, rows, expert, expert, expert),
        out_specs=(rows, rows, P("ep", "grp", None), P("ep", "grp", None), P("ep", None, "grp")),
        check_vma=False,
    )
```

time: 572 us -> 164 us (0.29); the launches traced: 566 us -> 164 us
  waiting for transfers between devices: 254 us -> 0 us
  starting transfers between devices: 156 us -> 0 us
  Pallas kernels: 0 us -> 153 us
  local copies, waits for them, and re-layouts: 68.6 us -> 10.3 us
  matrix products: 43.8 us -> 0 us
  other arithmetic: 28.3 us -> 0 us
  between operations: 14.7 us -> 0.65 us
    all_to_all x5 -> x0, waiting for transfers between devices: 254 us -> none  [the longest x1 90.8 us: shards(): lax.all_to_all(send_dy, 'ep', split_axis=0, concat_axis=0, tiled=True)]
    all_to_all x5 -> x0, starting transfers between devices: 156 us -> none  [the longest x1 123 us: shards(): lax.all_to_all(gk_slots, 'ep', split_axis=0, concat_axis=0, tiled=True)]
    pallas_call x0 -> x1, Pallas kernels: none -> 153 us  [shards(): pl.pallas_call(kernel, out_shape=(jax.ShapeDtypeStruct((tok, width), BF16...]
    gather x7 -> x0, local copies, waits for them, and re-layouts: 48.4 us -> none  [the longest x1 11.6 us: owner_blocks(): recv_dy.reshape(slot_count, row_width)[pick_row]]
    dot_general x22 -> x0, matrix products: 43.8 us -> none  [the longest x8 18.1 us: dot_plain(): return jnp.dot(left, right, preferred_element_type=jnp.float32)]
    select_n x6 -> x0, other arithmetic: 11.8 us -> none  [the longest x1 5.91 us: owner_blocks(): jnp.where(is_valid[:, None], recv_x.reshape(slot_count, row_width)[pick_r...]
    convert_element_type x6 -> x0, other arithmetic: 11.6 us -> none  [the longest x1 3.9 us: shards(): acc_down[None].astype(jnp.bfloat16)]
    unnamed x9, local copies, waits for them, and re-layouts: 0.83 us -> 10.3 us
  transfers between devices with their start and end apart: 8 -> 0, of which waited for: 5 -> 0; matrix products, arithmetic and copies ran while one was open for 12% -> 0% of each run, Pallas kernels for 0% -> 0%
where the time goes in v1:
time: 164 us
  Pallas kernels  153 us (93%)
  local copies, waits for them, and re-layouts  10.3 us (6%)
    pallas_call x1, Pallas kernels, shards(): pl.pallas_call(kernel, out_shape=(jax.ShapeDtypeStruct((tok, width), BF16...  153 us
    unnamed x9, local copies, waits for them, and re-layouts  10.3 us

profile of v1, /device:TPU:32, one launch (start us, length us, event | category | flops | bytes accessed | tf_op | source)
XLA Modules:
  0.0 163.9 jit_solution(4645280105430496037)
XLA Ops:
  0.6 1.4 copy.12.combine
  2.0 1.4 copy.13.expert_ids
  3.4 153.0 %shard_map.110 = (bf16[32,2048]{1,0:T(8,128)(2,1)}, bf16[32,10]{1,0:T(8,128)(2,1)}, bf16[512,512]{1,0:T(8,128)(2,1)}, bf16[512,512]{1,0:T(8,128)(2,1)}, bf16[512,512]{1,0:T(8,128)(2,1)}) custom-call(bf16[32,2048]{1,0:T(8,128)(2,1)} %tokens.1, bf16[32,2048]{1,0:T(8,128)(2,1)} %grad_out.1, bf16[32,10]{1,0:T(8,128)(2,1)} %copy.12.combine, ...), custom_call_target="tpu_custom_call" | custom-call | tf_op jit(solution)/shard_map/pallas_call | solution.py:597
  156.4 0.0 copy-start
  156.4 1.4 copy.14
  157.8 1.6 copy.19
  159.4 1.9 %copy.20 = bf16[1,512,512]{2,1,0:T(8,128)(2,1)} copy(bf16[1,512,512]{2,1,0:T(8,128)(2,1)} %bitcast.11) | data formatting | bytes 1048576
  161.2 1.9 %copy.21 = bf16[1,512,512]{2,1,0:T(8,128)(2,1)} copy(bf16[1,512,512]{2,1,0:T(8,128)(2,1)} %bitcast.10) | data formatting | bytes 1048576
  163.1 0.0 copy-done
  163.1 0.8 copy.22
Async XLA Ops:
  156.4 6.7 %copy-start = (bf16[512,512]{1,0:T(8,128)(2,1)S(1)}, bf16[512,512]{1,0:T(8,128)(2,1)}, u32[]{:S(2)}) copy-start(bf16[512,512]{1,0:T(8,128)(2,1)} %get-tuple-element.14) | copy-start | bytes 1572868

commit v2 on v1

--- a/solution.py
+++ b/solution.py
@@ -22,16 +22,63 @@
 CHUNK = 8
 CTOK = CHUNK * TOK
 CROW = CHUNK * CAP
-ROUNDS = 2 * BLOCKS // CHUNK
+ROUNDS = BLOCKS // CHUNK
+
+
+ORDER = (
+    (
+        *((0, 0), (1, 0), (-1, 0), (2, 0), (0, 1), (0, -1), (1, 1), (1, -1)),
+        *((-1, 1), (-1, -1), (2, 1), (2, -1), (0, 2), (0, -2), (1, 2), (1, -2)),
+        *((-1, 2), (-1, -2), (2, 2), (2, -2), (0, 3), (0, -3), (1, 3), (1, -3)),
+        *((-1, 3), (-1, -3), (2, 3), (2, -3), (-1, 4), (1, 4), (0, 4), (2, 4)),
+    ),
+    (
+        *((0, 0), (0, 1), (0, -1), (1, 0), (-1, 0), (0, 2), (0, -2), (1, 1)),
+        *((-1, 1), (1, -1), (-1, -1), (0, 3), (0, -3), (2, 0), (1, 2), (-1, 2)),
+        *((1, -2), (-1, -2), (0, 4), (2, 1), (2, -1), (1, 3), (-1, 3), (1, -3)),
+        *((-1, -3), (1, 4), (-1, 4), (2, 2), (2, -2), (2, 3), (2, -3), (2, 4)),
+    ),
+)
 
 
 def slot_of(kind, ox, oz):
-    xi, zi = XO.index(ox), ZO.index(oz)
-    return zi * NX + xi if kind == 0 else xi * NZ + zi
+    return ORDER[kind].index((ox, oz))
+
+
+def children(kind, ox, oz, half):
+    found = []
+    if kind == 0 and oz == 0 or kind == 1:
+        if ox == 0:
+            found += [((1, oz), 0), ((-1, oz), 1)]
+        elif (ox, half) == (1, 0):
+            found.append(((2, oz), 0))
+        elif (ox, half) == (-1, 1):
+            found.append(((2, oz), 1))
+    elif (ox, half) == (1, 0) and oz in (-2, 3, -3, 4):
+        found.append(((2, oz), 0))
+    elif (ox, half) == (-1, 1) and oz in (2, 3, -3, 4):
+        found.append(((2, oz), 1))
+    along_z = ox == 0 if kind == 1 else ox != 2 or oz == 0 or (oz, half) in ((1, 0), (-1, 1))
+    if along_z:
+        if oz == 0:
+            found += [((ox, 1), 2), ((ox, -1), 3)]
+        elif oz in (1, 2) or (oz, half) == (3, 0):
+            found.append(((ox, oz + 1), 2))
+        elif oz in (-1, -2):
+            found.append(((ox, oz - 1), 3))
+        elif (oz, half) == (-3, 1):
+            found.append(((ox, 4), 3))
+    return found
 
 
 def dot(left, right, dims=((1,), (0,))):
     return lax.dot_general(left, right, (dims, ((), ())), preferred_element_type=F32)
+
+
+def identity(size):
+    row = lax.broadcasted_iota(jnp.int32, (size, size), 0)
+    col = lax.broadcasted_iota(jnp.int32, (size, size), 1)
+    return (row == col).astype(F32).astype(BF16)
 
 
 def kernel(
@@ -110,12 +157,14 @@
     ]
     for load in loads:
         load.start()
-    lane_iota = lax.broadcasted_iota(jnp.int32, (TOK, LANES), 1)
-    ids = expert_ids[...]
+    top = expert_ids.shape[0]
+    expert_iota = lax.broadcasted_iota(jnp.int32, (LANES, TOK), 0)
     weights = combine[...].astype(F32)
-    table = jnp.zeros((TOK, LANES), F32)
-    for k in range(ids.shape[1]):
-        table = table + jnp.where(ids[:, k : k + 1] == lane_iota, weights[:, k : k + 1], 0.0)
+    table = jnp.zeros((LANES, TOK), F32)
+    for k in range(top):
+        named = expert_ids[k : k + 1, :] == expert_iota
+        table = table + jnp.where(named, weights[k : k + 1, :], 0.0)
+    table = dot(identity(TOK), table.astype(BF16), ((1,), (1,)))
     buf[core, 0:TOK, 2 * width : 2 * width + LANES] = table.astype(BF16)
     loads[0].wait()
     loads[1].wait()
@@ -128,9 +177,9 @@
             return pl.ds(slot * TOK, TOK)
         return pl.ds(slot * TOK + half * HALF, HALF)
 
-    def hop(kind, source, target, other, half=None):
+    def hop(kind, source, target, other, half):
         a, b = slot_of(kind, *source), slot_of(kind, *target)
-        index = (kind * BLOCKS + b) * 2 + (half or 0)
+        index = (kind * BLOCKS + b) * 2 + half
         return pltpu.make_async_remote_copy(
             src_ref=buf.at[kind, span(a, half)],
             dst_ref=buf.at[kind, span(b, half)],
@@ -139,10 +188,6 @@
             device_id=other,
             device_id_type=MESH,
         )
-
-    def send(kind, source, target, other, half=None):
-        hop(kind, source, target, other, half).start()
-        hops[kind][target, half] = source, other
 
     def across(kind, slot):
         return pltpu.make_async_remote_copy(
@@ -154,154 +199,78 @@
             device_id_type=MESH,
         )
 
+    def forward(kind, offset, half):
+        for target, way in children(kind, *offset, half):
+            other = (x_next, x_prev, z_next, z_prev)[way]
+            hop(kind, offset, target, other, half).start()
+            hops[kind][target, half] = offset, other
+
     def share(kind, offset):
         across(kind, slot_of(kind, *offset)).start()
         shares[kind][offset] = True
 
-    def arrive(kind, offset, half=None):
-        hop(kind, offset, offset, z_next, half).wait_recv()
-
-    def z_out(kind, ox, oz):
-        if oz == 0:
-            send(kind, (ox, 0), (ox, 1), z_next)
-            send(kind, (ox, 0), (ox, -1), z_prev)
-        elif oz == 3:
-            send(kind, (ox, 3), (ox, 4), z_next, half=0)
-        elif oz == -3:
-            send(kind, (ox, -3), (ox, 4), z_prev, half=1)
-        elif oz > 0:
-            send(kind, (ox, oz), (ox, oz + 1), z_next)
-        else:
-            send(kind, (ox, oz), (ox, oz - 1), z_prev)
-
-    def x_out(oz):
-        send(1, (0, oz), (1, oz), x_next)
-        send(1, (0, oz), (-1, oz), x_prev)
-
-    def first_round(kind):
-        if kind == 0:
-            send(0, (0, 0), (1, 0), x_next)
-            send(0, (0, 0), (-1, 0), x_prev)
-            z_out(0, 0, 0)
-            share(0, (0, 0))
-            arrive(0, (1, 0))
-            send(0, (1, 0), (2, 0), x_next, half=0)
-            z_out(0, 1, 0)
-            share(0, (1, 0))
-            arrive(0, (-1, 0))
-            send(0, (-1, 0), (2, 0), x_prev, half=1)
-            z_out(0, -1, 0)
-            share(0, (-1, 0))
-            arrive(0, (2, 0), 0)
-            arrive(0, (2, 0), 1)
-            z_out(0, 2, 0)
-            share(0, (2, 0))
-            z_round(1)
-        else:
-            z_out(1, 0, 0)
-            x_out(0)
-            share(1, (0, 0))
-            for oz in (1, -1, 2, -2):
-                arrive(1, (0, oz))
-                z_out(1, 0, oz)
-                x_out(oz)
-                share(1, (0, oz))
-
-    def z_round(k):
-        for ox in XO:
-            for oz in (k, -k):
-                arrive(0, (ox, oz))
-                z_out(0, ox, oz)
-                share(0, (ox, oz))
-
-    def z_last():
-        for ox in XO:
-            arrive(0, (ox, 4), 0)
-            arrive(0, (ox, 4), 1)
-            share(0, (ox, 4))
-
-    def x_near(offsets):
-        for oz in offsets:
-            even = ZO.index(oz) % 2 == 0
-            arrive(1, (1, oz))
-            if even:
-                send(1, (1, oz), (2, oz), x_next)
-            share(1, (1, oz))
-            arrive(1, (-1, oz))
-            if not even:
-                send(1, (-1, oz), (2, oz), x_prev)
-            share(1, (-1, oz))
-
-    def x_far(offsets):
-        for oz in offsets:
-            arrive(1, (2, oz))
-            share(1, (2, oz))
-
-    def second_round():
-        for oz in (3, -3):
-            arrive(1, (0, oz))
-            z_out(1, 0, oz)
-            x_out(oz)
-            share(1, (0, oz))
-        x_near((0,))
-        arrive(1, (0, 4), 0)
-        arrive(1, (0, 4), 1)
-        x_out(4)
-        share(1, (0, 4))
-
-    plans = (
-        {
-            0: lambda: first_round(0),
-            2: lambda: z_round(2),
-            4: lambda: z_round(3),
-            6: z_last,
-        },
-        {
-            0: lambda: first_round(1),
-            1: second_round,
-            2: lambda: x_near((1, -1, 2, -2)),
-            3: lambda: x_near((3, -3, 4)),
-            5: lambda: x_far((0, 1, -1)),
-            6: lambda: x_far((2, -2)),
-            7: lambda: x_far((3, -3, 4)),
-        },
-    )
-
-    def pair_copy(kind, rows):
+    def serve(kind, offset):
+        for half in range(2):
+            if offset != (0, 0):
+                hop(kind, offset, offset, z_next, half).wait_recv()
+            forward(kind, offset, half)
+        share(kind, offset)
+
+    def serve_all(step, kind, offsets):
+        @pl.when((step == 0) & (core == kind))
+        def _():
+            for offset in offsets:
+                serve(kind, offset)
+
+    def service(step, place):
+        for kind in range(2):
+            for r in range(1, ROUNDS):
+
+                @pl.when((step == r - 1) & (core == kind))
+                def _(kind=kind, r=r):
+                    serve(kind, ORDER[kind][r * CHUNK + place])
+
+    def pair_copy(kind, rows, step):
         return pltpu.make_async_remote_copy(
             src_ref=grads.at[kind, rows],
             dst_ref=sib.at[rows],
-            send_sem=sib_send.at[rows.start // CTOK],
-            recv_sem=sib_recv.at[rows.start // CTOK],
+            send_sem=sib_send.at[step],
+            recv_sem=sib_recv.at[step],
             device_id=sibling,
             device_id_type=MESH,
         )
 
-    def chunk(step, kind):
-        first = pl.multiple_of((step // 2) * CTOK, CTOK)
-        rows = pl.ds(first, CTOK)
-        packed = pl.ds(pl.multiple_of(step * CROW, CROW), CROW)
+    def chunk(step):
+        rows = pl.ds(pl.multiple_of(step * CTOK, CTOK), CTOK)
+        first = pl.multiple_of(step * 2 * CROW, 2 * CROW)
+        packed = pl.ds(first, 2 * CROW)
         pick = (lax.broadcasted_iota(jnp.int32, (CAP, LANES), 1) == me).astype(F32).astype(BF16)
-        table = buf[kind, rows, 2 * width : 2 * width + LANES]
-        weight_row = dot(pick, table, ((1,), (1,)))
-        routed = jnp.where(weight_row > 0, 1.0, 0.0)
         row_id = lax.broadcasted_iota(jnp.int32, (CTOK, CTOK), 0)
         col_id = lax.broadcasted_iota(jnp.int32, (CTOK, CTOK), 1)
         upto = (row_id <= col_id) & (row_id // TOK == col_id // TOK)
-        rank = dot(routed.astype(BF16), upto.astype(F32).astype(BF16))
+        upto = upto.astype(F32).astype(BF16)
         base = (lax.broadcasted_iota(jnp.int32, (1, CTOK), 1) // TOK * CAP).astype(F32)
-        target = jnp.where(routed[0:1] > 0, base + rank[0:1] - 1.0, -1.0)
         place = lax.broadcasted_iota(jnp.int32, (CROW, CTOK), 0).astype(F32)
-        select = jnp.where(place == target, 1.0, 0.0)
-        weight = jnp.sum(select * weight_row[0:1], axis=1, keepdims=True)
-        select_t = select.T.astype(BF16)
-        select = select.astype(BF16)
-        for c in range(2 * NG):
-            cols = slice((c % NG) * part, (c % NG + 1) * part)
-            picked = dot(select, buf[kind, rows, c * part : (c + 1) * part])
-            rows_all[c // NG, packed, cols] = picked.astype(BF16)
-
-        combine_grad = jnp.zeros((CROW, 1), F32)
+        weight_parts, back_select = [], []
+        for kind in range(2):
+            table = buf[kind, rows, 2 * width : 2 * width + LANES]
+            weight_row = dot(pick, table, ((1,), (1,)))
+            routed = jnp.where(weight_row > 0, 1.0, 0.0)
+            rank = dot(routed.astype(BF16), upto)
+            target = jnp.where(routed[0:1] > 0, base + rank[0:1] - 1.0, -1.0)
+            select = jnp.where(place == target, 1.0, 0.0)
+            weight_parts.append(jnp.sum(select * weight_row[0:1], axis=1, keepdims=True))
+            back_select.append(select.T.astype(BF16))
+            select = select.astype(BF16)
+            own = pl.ds(pl.multiple_of(first + kind * CROW, CROW), CROW)
+            for c in range(2 * NG):
+                cols = slice((c % NG) * part, (c % NG + 1) * part)
+                picked = dot(select, buf[kind, rows, c * part : (c + 1) * part])
+                rows_all[c // NG, own, cols] = picked.astype(BF16)
+            service(step, kind)
+        weight = jnp.concatenate(weight_parts, axis=0)
+
+        combine_grad = jnp.zeros((2 * CROW, 1), F32)
         for f in range(2):
             cols = slice(f * fhalf, (f + 1) * fhalf)
             x_rows = rows_all[0, packed, :]
@@ -321,49 +290,65 @@
             rows_t[0, cols, packed] = gate_rows.T.astype(BF16)
             rows_t[1, cols, packed] = up_rows.T.astype(BF16)
             rows_t[2, cols, packed] = (hidden * weight).T.astype(BF16)
+            service(step, 2 + f)
 
         for c in range(NG):
             cols = slice(c * part, (c + 1) * part)
             row_grad = dot(pair[0], wg[cols, :], ((1,), (1,)))
             row_grad = row_grad + dot(pair[1], wu[cols, :], ((1,), (1,)))
-            grads[kind, rows, cols] = dot(select_t, row_grad.astype(BF16)).astype(BF16)
-        lanes = lax.broadcasted_iota(jnp.int32, (CROW, LANES), 1)
+            row_grad = row_grad.astype(BF16)
+            for kind in range(2):
+                mine = row_grad[kind * CROW : (kind + 1) * CROW]
+                grads[kind, rows, cols] = dot(back_select[kind], mine).astype(BF16)
+            service(step, 4 + c)
+        lanes = lax.broadcasted_iota(jnp.int32, (2 * CROW, LANES), 1)
         spread = jnp.where(lanes == me, combine_grad, 0.0).astype(BF16)
-        grads[kind, rows, width:grad_width] = dot(select_t, spread).astype(BF16)
-        return rows
+        for kind in range(2):
+            mine = spread[kind * CROW : (kind + 1) * CROW]
+            grads[kind, rows, width:grad_width] = dot(back_select[kind], mine).astype(BF16)
+
+    def pair_sum(step):
+        first = pl.multiple_of(step * CTOK, CTOK)
+        pair_copy(core, pl.ds(first, CTOK), step).wait_recv()
+
+        def piece(j, carry):
+            rows = pl.ds(pl.multiple_of(first + j * TOK, TOK), TOK)
+            total = grads[core, rows, :].astype(F32) + sib[rows, :].astype(F32)
+            grads[core, rows, :] = total.astype(BF16)
+            return carry
+
+        lax.fori_loop(0, CHUNK, piece, 0)
 
     def round_body(step, carry):
-        kind = step % 2
-        for c in range(2):
-            for r, plan in plans[c].items():
-                pl.when((step == r) & (core == c))(plan)
-
-        @pl.when(kind != core)
-        def _():
-            def wait_block(i, carry):
-                slot = (step // 2) * CHUNK + i
-                pltpu.make_async_remote_copy(
-                    src_ref=buf.at[kind, pl.ds(pl.multiple_of(slot * TOK, TOK), TOK)],
-                    dst_ref=buf.at[kind, pl.ds(pl.multiple_of(slot * TOK, TOK), TOK)],
-                    send_sem=core_send.at[slot],
-                    recv_sem=ag_recv.at[(kind * BLOCKS + slot) * 2],
-                    device_id=sibling,
-                    device_id_type=MESH,
-                ).wait_recv()
-                return carry
-
-            lax.fori_loop(0, CHUNK, wait_block, 0)
+        for kind in range(2):
+            serve_all(step, kind, ORDER[kind][:CHUNK])
+
+        def wait_block(i, inner):
+            slot = step * CHUNK + i
+            rows = pl.ds(pl.multiple_of(slot * TOK, TOK), TOK)
+            pltpu.make_async_remote_copy(
+                src_ref=buf.at[1 - core, rows],
+                dst_ref=buf.at[1 - core, rows],
+                send_sem=core_send.at[slot],
+                recv_sem=ag_recv.at[((1 - core) * BLOCKS + slot) * 2],
+                device_id=sibling,
+                device_id_type=MESH,
+            ).wait_recv()
+            return inner
+
+        lax.fori_loop(0, CHUNK, wait_block, 0)
 
         @pl.when(step == 0)
         def _():
             for load in loads[2:]:
                 load.wait()
 
-        rows = chunk(step, kind)
-
-        @pl.when(kind != core)
+        chunk(step)
+        pair_copy(1 - core, pl.ds(pl.multiple_of(step * CTOK, CTOK), CTOK), step).start()
+
+        @pl.when(step > 0)
         def _():
-            pair_copy(kind, rows).start()
+            pair_sum(step - 1)
 
         return carry
 
@@ -464,22 +449,6 @@
         copy.start()
         rs_sent.append(copy)
 
-    def pair_sums():
-        def body(i, carry):
-            rows = pl.ds(pl.multiple_of(i * CTOK, CTOK), CTOK)
-            copy = pair_copy(core, rows)
-            copy.wait_recv()
-
-            def piece(j, inner):
-                part_rows = pl.ds(pl.multiple_of(i * CTOK + j * TOK, TOK), TOK)
-                total = grads[core, part_rows, :].astype(F32) + sib[part_rows, :].astype(F32)
-                grads[core, part_rows, :] = total.astype(BF16)
-                return inner
-
-            return lax.fori_loop(0, CHUNK, piece, carry)
-
-        lax.fori_loop(0, BLOCKS // CHUNK, body, 0)
-
     zi_order = (7, 5, 6, 3, 4, 1, 2, 0)
 
     def x_start():
@@ -529,21 +498,16 @@
         z_copy(1, 1).wait_recv()
         total = total + znear[0].astype(F32) + znear[4].astype(F32)
         o_tokens[...] = total[:, :width].astype(BF16)
-        by_expert = total[:, width:grad_width]
-        column = lax.broadcasted_iota(jnp.int32, o_combine.shape, 1)
-        out = jnp.zeros(o_combine.shape, F32)
-        for k in range(o_combine.shape[1]):
-            value = jnp.sum(
-                jnp.where(expert_ids[:, k : k + 1] == lane_iota, by_expert, 0.0),
-                axis=1,
-                keepdims=True,
-            )
-            out = out + jnp.where(column == k, value, 0.0)
-        o_combine[...] = out.astype(BF16)
+        by_expert = total[:, width:grad_width].astype(BF16)
+        by_expert = dot(identity(LANES), by_expert, ((1,), (1,)))
+        for k in range(top):
+            named = expert_ids[k : k + 1, :] == expert_iota
+            value = jnp.sum(jnp.where(named, by_expert, 0.0), axis=0, keepdims=True)
+            o_combine[k : k + 1, :] = value.astype(BF16)
 
     for mat in range(3):
         y_task(0, mat)
-    pair_sums()
+    pair_sum(ROUNDS - 1)
     x_start()
     y_task(1, 0)
     y_task(1, 1)
@@ -575,12 +539,25 @@
                 across(kind, slot_of(kind, *offset)).wait_send()
 
     def pair_done(i, carry):
-        pair_copy(1 - core, pl.ds(pl.multiple_of(i * CTOK, CTOK), CTOK)).wait_send()
+        pair_copy(1 - core, pl.ds(pl.multiple_of(i * CTOK, CTOK), CTOK), i).wait_send()
         return carry
 
     lax.fori_loop(0, BLOCKS // CHUNK, pair_done, 0)
     for copy in y_sent + rs_sent:
         copy.wait_send()
+
+
+def hand_out(*refs):
+    sources, targets, held, sems = refs[:5], refs[5:10], refs[10:15], refs[15]
+    taken = [pltpu.make_async_copy(sources[i], held[i], sems.at[i]) for i in range(5)]
+    given = [pltpu.make_async_copy(held[i], targets[i], sems.at[5 + i]) for i in range(5)]
+    for copy in taken:
+        copy.start()
+    for before, after in zip(taken, given):
+        before.wait()
+        after.start()
+    for copy in given:
+        copy.wait()
 
 
 def shards(tokens, grad_out, combine, expert_ids, w_gate, w_up, w_down):
@@ -589,7 +566,7 @@
     ff = w_gate.shape[2]
     part = width // NG
     slots = BLOCKS * TOK
-    picked = ROUNDS * CROW
+    picked = 2 * ROUNDS * CROW
     gw = width + LANES
     any_spec = pl.BlockSpec(memory_space=pl.ANY)
     vmem_spec = pl.BlockSpec(memory_space=pltpu.VMEM)
@@ -598,7 +575,7 @@
         kernel,
         out_shape=(
             jax.ShapeDtypeStruct((tok, width), BF16),
-            jax.ShapeDtypeStruct((tok, top), BF16),
+            jax.ShapeDtypeStruct((top, tok), BF16),
             jax.ShapeDtypeStruct((part, ff), BF16),
             jax.ShapeDtypeStruct((part, ff), BF16),
             jax.ShapeDtypeStruct((ff, part), BF16),
@@ -612,7 +589,7 @@
             pltpu.VMEM((ff, width), BF16),
             pltpu.VMEM((2, picked, width), BF16),
             pltpu.VMEM((3, ff, picked), BF16),
-            pltpu.VMEM((2, CROW, ff), BF16),
+            pltpu.VMEM((2, 2 * CROW, ff), BF16),
             pltpu.VMEM((2, slots, gw), BF16),
             pltpu.VMEM((slots, gw), BF16),
             pltpu.VMEM((6, ff // 2, part), BF16),
@@ -638,9 +615,16 @@
         compiler_params=pltpu.CompilerParams(
             collective_id=0, has_side_effects=True, vmem_limit_bytes=63 << 20
         ),
-    )(tokens, grad_out, combine, expert_ids, w_gate[0], w_up[0], w_down[0])
+    )(tokens, grad_out, combine.T, expert_ids.T, w_gate[0], w_up[0], w_down[0])
+    results = pl.pallas_call(
+        hand_out,
+        out_shape=tuple(jax.ShapeDtypeStruct(r.shape, r.dtype) for r in results),
+        in_specs=[any_spec] * 5,
+        out_specs=[any_spec] * 5,
+        scratch_shapes=[pltpu.VMEM(r.shape, r.dtype) for r in results] + [dma((10,))],
+    )(*results)
     g_tokens, g_combine, g_gate, g_up, g_down = results
-    return g_tokens, g_combine, g_gate[None], g_up[None], g_down[None]
+    return g_tokens, g_combine.T, g_gate[None], g_up[None], g_down[None]
 
 
 def solution(mesh):

time: 164 us -> 141 us (0.86); the launches traced: 164 us -> 138 us
  Pallas kernels: 153 us -> 137 us
  local copies, waits for them, and re-layouts: 10.3 us -> 0 us
    pallas_call x1, Pallas kernels: 153 us -> 135 us  [shards(): pl.pallas_call(kernel, out_shape=(jax.ShapeDtypeStruct((tok, width), BF16...]
    unnamed x9 -> x0, local copies, waits for them, and re-layouts: 10.3 us -> none
    pallas_call x0 -> x1, Pallas kernels: none -> 2.35 us  [shards(): pl.pallas_call(hand_out, out_shape=tuple((jax.ShapeDtypeStruct(r.shape, r...]
where the time goes in v2:
time: 141 us; the launch traced here: 138 us
  Pallas kernels  137 us (97%)
    pallas_call x1, Pallas kernels, shards(): pl.pallas_call(kernel, out_shape=(jax.ShapeDtypeStruct((tok, width), BF16...  135 us

profile of v2, /device:TPU:32, one launch (start us, length us, event | category | flops | bytes accessed | tf_op | source)
XLA Modules:
  0.0 138.0 jit_solution(16136901541783454007)
XLA Ops:
  0.6 134.8 %shard_map.110 = (bf16[32,2048]{1,0:T(8,128)(2,1)}, bf16[10,32]{1,0:T(8,128)(2,1)}, bf16[512,512]{1,0:T(8,128)(2,1)}, bf16[512,512]{1,0:T(8,128)(2,1)}, bf16[512,512]{1,0:T(8,128)(2,1)}) custom-call(bf16[32,2048]{1,0:T(8,128)(2,1)} %tokens.1, bf16[32,2048]{1,0:T(8,128)(2,1)} %grad_out.1, bf16[10,32]{1,0:T(8,128)(2,1)} %bitcast.13, s32[10,32]{1,0:T(8,128)} %bitcast.12, ...), custom_call_target="tpu_custom_call" | custom-call | tf_op jit(solution)/shard_map/pallas_call | solution.py:574
  135.4 2.3 %shard_map.111 = (bf16[32,2048]{1,0:T(8,128)(2,1)}, bf16[10,32]{1,0:T(8,128)(2,1)}, bf16[512,512]{1,0:T(8,128)(2,1)}, bf16[512,512]{1,0:T(8,128)(2,1)}, bf16[512,512]{1,0:T(8,128)(2,1)}) custom-call(bf16[32,2048]{1,0:T(8,128)(2,1)} %get-tuple-element.15.refs_0_, bf16[10,32]{1,0:T(8,128)(2,1)} %get-tuple-element.16.refs_1_, ...), custom_call_target="tpu_custom_call" | custom-call | tf_op jit(solution)/shard_map/pallas_call | solution.py:619

commit v3 on v2

--- a/solution.py
+++ b/solution.py
@@ -27,18 +27,29 @@
 
 ORDER = (
     (
-        *((0, 0), (1, 0), (-1, 0), (2, 0), (0, 1), (0, -1), (1, 1), (1, -1)),
-        *((-1, 1), (-1, -1), (2, 1), (2, -1), (0, 2), (0, -2), (1, 2), (1, -2)),
-        *((-1, 2), (-1, -2), (2, 2), (2, -2), (0, 3), (0, -3), (1, 3), (1, -3)),
-        *((-1, 3), (-1, -3), (2, 3), (2, -3), (-1, 4), (1, 4), (0, 4), (2, 4)),
+        *((0, 0), (1, 0), (0, 1), (1, -1), (0, -1), (0, 2), (-1, -1), (1, 1)),
+        *((0, -2), (-1, -2), (0, 3), (1, 2), (0, -3), (2, 0), (-1, 1), (2, -1)),
+        *((2, 1), (-1, -3), (-1, 0), (0, 4), (1, -2), (-1, 2), (1, 3), (2, 2)),
+        *((2, -3), (-1, 3), (-1, 4), (1, 4), (2, 3), (2, -2), (1, -3), (2, 4)),
     ),
     (
-        *((0, 0), (0, 1), (0, -1), (1, 0), (-1, 0), (0, 2), (0, -2), (1, 1)),
-        *((-1, 1), (1, -1), (-1, -1), (0, 3), (0, -3), (2, 0), (1, 2), (-1, 2)),
-        *((1, -2), (-1, -2), (0, 4), (2, 1), (2, -1), (1, 3), (-1, 3), (1, -3)),
-        *((-1, -3), (1, 4), (-1, 4), (2, 2), (2, -2), (2, 3), (2, -3), (2, 4)),
+        *((0, 0), (0, 1), (0, -1), (-1, 0), (0, 2), (-1, 1), (0, -2), (1, -1)),
+        *((1, 1), (0, -3), (0, 3), (2, -1), (1, 0), (1, 2), (1, -2), (-1, -2)),
+        *((-1, 2), (2, 1), (0, 4), (1, 3), (2, -2), (-1, 3), (-1, -1), (-1, -3)),
+        *((1, -3), (2, 0), (2, 2), (-1, 4), (2, 3), (2, -3), (1, 4), (2, 4)),
     ),
 )
+WAYS = (
+    (
+        (-1, 0, 2, 3, 3, 2, 1, 2, 3, 3, 2, 2, 3, 0, 1, 1, 0, 3, 1, 2, 3, 2, 2, 0, 1, 1, 3, 2, 0, 2, 3, 0),
+        (-1, 0, 2, 3, 3, 2, 1, 0, 3, 3, 2, 2, 3, 0, 1, 1, 0, 3, 1, 3, 0, 2, 0, 0, 1, 2, 3, 2, 0, 2, 1, 3),
+    ),
+    (
+        (-1, 2, 3, 1, 2, 1, 3, 0, 0, 3, 2, 0, 2, 2, 0, 1, 1, 0, 2, 2, 1, 1, 0, 1, 3, 3, 2, 1, 0, 1, 3, 2),
+        (-1, 2, 3, 1, 2, 1, 3, 0, 0, 3, 2, 0, 0, 0, 0, 1, 1, 1, 3, 0, 1, 2, 0, 1, 3, 3, 1, 1, 0, 0, 3, 1),
+    ),
+)
+MOVES = ((1, 0), (-1, 0), (0, 1), (0, -1))
 
 
 def slot_of(kind, ox, oz):
@@ -47,27 +58,10 @@
 
 def children(kind, ox, oz, half):
     found = []
-    if kind == 0 and oz == 0 or kind == 1:
-        if ox == 0:
-            found += [((1, oz), 0), ((-1, oz), 1)]
-        elif (ox, half) == (1, 0):
-            found.append(((2, oz), 0))
-        elif (ox, half) == (-1, 1):
-            found.append(((2, oz), 1))
-    elif (ox, half) == (1, 0) and oz in (-2, 3, -3, 4):
-        found.append(((2, oz), 0))
-    elif (ox, half) == (-1, 1) and oz in (2, 3, -3, 4):
-        found.append(((2, oz), 1))
-    along_z = ox == 0 if kind == 1 else ox != 2 or oz == 0 or (oz, half) in ((1, 0), (-1, 1))
-    if along_z:
-        if oz == 0:
-            found += [((ox, 1), 2), ((ox, -1), 3)]
-        elif oz in (1, 2) or (oz, half) == (3, 0):
-            found.append(((ox, oz + 1), 2))
-        elif oz in (-1, -2):
-            found.append(((ox, oz - 1), 3))
-        elif (oz, half) == (-3, 1):
-            found.append(((ox, 4), 3))
+    for target, way in zip(ORDER[kind], WAYS[kind][half]):
+        dx, dz = MOVES[way]
+        if way >= 0 and (target[0] - ox - dx) % NX == 0 and (target[1] - oz - dz) % NZ == 0:
+            found.append((target, way))
     return found
 
 
@@ -101,6 +95,8 @@
     rows_all,
     rows_t,
     pair,
+    back_select,
+    spread,
     grads,
     sib,
     ysend,
@@ -240,7 +236,7 @@
             device_id_type=MESH,
         )
 
-    def chunk(step):
+    def ahead(step):
         rows = pl.ds(pl.multiple_of(step * CTOK, CTOK), CTOK)
         first = pl.multiple_of(step * 2 * CROW, 2 * CROW)
         packed = pl.ds(first, 2 * CROW)
@@ -251,7 +247,7 @@
         upto = upto.astype(F32).astype(BF16)
         base = (lax.broadcasted_iota(jnp.int32, (1, CTOK), 1) // TOK * CAP).astype(F32)
         place = lax.broadcasted_iota(jnp.int32, (CROW, CTOK), 0).astype(F32)
-        weight_parts, back_select = [], []
+        weight_parts = []
         for kind in range(2):
             table = buf[kind, rows, 2 * width : 2 * width + LANES]
             weight_row = dot(pick, table, ((1,), (1,)))
@@ -260,7 +256,7 @@
             target = jnp.where(routed[0:1] > 0, base + rank[0:1] - 1.0, -1.0)
             select = jnp.where(place == target, 1.0, 0.0)
             weight_parts.append(jnp.sum(select * weight_row[0:1], axis=1, keepdims=True))
-            back_select.append(select.T.astype(BF16))
+            back_select[kind] = select.T.astype(BF16)
             select = select.astype(BF16)
             own = pl.ds(pl.multiple_of(first + kind * CROW, CROW), CROW)
             for c in range(2 * NG):
@@ -292,6 +288,12 @@
             rows_t[2, cols, packed] = (hidden * weight).T.astype(BF16)
             service(step, 2 + f)
 
+        lanes = lax.broadcasted_iota(jnp.int32, (2 * CROW, LANES), 1)
+        spread[...] = jnp.where(lanes == me, combine_grad, 0.0).astype(BF16)
+
+    def behind(step, serving):
+        first = pl.multiple_of(step * CTOK, CTOK)
+        rows = pl.ds(first, CTOK)
         for c in range(NG):
             cols = slice(c * part, (c + 1) * part)
             row_grad = dot(pair[0], wg[cols, :], ((1,), (1,)))
@@ -300,12 +302,12 @@
             for kind in range(2):
                 mine = row_grad[kind * CROW : (kind + 1) * CROW]
                 grads[kind, rows, cols] = dot(back_select[kind], mine).astype(BF16)
-            service(step, 4 + c)
-        lanes = lax.broadcasted_iota(jnp.int32, (2 * CROW, LANES), 1)
-        spread = jnp.where(lanes == me, combine_grad, 0.0).astype(BF16)
+            if serving:
+                service(step, 4 + c)
         for kind in range(2):
-            mine = spread[kind * CROW : (kind + 1) * CROW]
+            mine = spread[kind * CROW : (kind + 1) * CROW, :]
             grads[kind, rows, width:grad_width] = dot(back_select[kind], mine).astype(BF16)
+        pair_copy(1 - core, rows, step).start()
 
     def pair_sum(step):
         first = pl.multiple_of(step * CTOK, CTOK)
@@ -343,10 +345,13 @@
             for load in loads[2:]:
                 load.wait()
 
-        chunk(step)
-        pair_copy(1 - core, pl.ds(pl.multiple_of(step * CTOK, CTOK), CTOK), step).start()
-
-        @pl.when(step > 0)
+        ahead(step)
+
+        @pl.when(step < ROUNDS - 1)
+        def _():
+            behind(step, True)
+
+        @pl.when((step > 0) & (step < ROUNDS - 1))
         def _():
             pair_sum(step - 1)
 
@@ -419,29 +424,25 @@
         )
 
     def far_copy(zi):
-        oz = ZO[zi]
-        other = x_prev if zi % 2 == 0 else x_next
-        return push(block(2, oz), xfar.at[zi], xf_send.at[zi], xf_recv.at[zi], other)
-
-    def near_copy(side, zi):
-        oz = ZO[zi]
-        index = side * NZ + zi
-        other = x_prev if side == 0 else x_next
+        return push(block(2, ZO[zi]), xfar.at[zi], xf_send.at[zi], xf_recv.at[zi], x_prev)
+
+    def near_copy(zi):
+        return push(block(-1, ZO[zi]), xnear.at[zi], xn_send.at[zi], xn_recv.at[zi], x_next)
+
+    def last_copy():
+        return push(block(1, 0), xnear.at[NZ], xn_send.at[NZ], xn_recv.at[NZ], x_prev)
+
+    def z_copy(ox, side, k):
+        index = (ox * 2 + side) * 4 + k - 1
+        if k == 4:
+            source = block(ox, 4, side)
+            target = znear.at[index, pl.ds(side * HALF, HALF)]
+        else:
+            source = block(ox, (1 - 2 * side) * k)
+            target = znear.at[index]
         return push(
-            block(1 - 2 * side, oz), xnear.at[index], xn_send.at[index], xn_recv.at[index], other
+            source, target, z_send.at[index], z_recv.at[index], z_prev if side == 0 else z_next
         )
-
-    def z_copy(side, k):
-        sign = 1 - 2 * side
-        other = z_prev if side == 0 else z_next
-        index = side * 4 + k - 1
-        target = znear.at[index]
-        half = None
-        if k == 4:
-            half = side
-            target = znear.at[index, pl.ds(side * HALF, HALF)]
-        oz = 4 if k == 4 else sign * k
-        return push(block(0, oz, half), target, z_send.at[index], z_recv.at[index], other)
 
     rs_sent = []
 
@@ -449,54 +450,58 @@
         copy.start()
         rs_sent.append(copy)
 
-    zi_order = (7, 5, 6, 3, 4, 1, 2, 0)
-
     def x_start():
-        for zi in zi_order:
+        for zi in (7, 5, 6, 3, 4, 1, 2, 0):
             go(far_copy(zi))
-        for zi in zi_order:
-            go(near_copy(1 if zi % 2 == 0 else 0, zi))
-
-    def x_add(zis):
-        for zi in zis:
-            side = 0 if zi % 2 == 0 else 1
-            far_copy(zi).wait_recv()
-            mine = block(1 - 2 * side, ZO[zi])
-            mine[...] = (mine[...].astype(F32) + xfar[zi].astype(F32)).astype(BF16)
-            go(near_copy(side, zi))
-
-    def x_total(oz):
+            go(near_copy(zi))
+
+    def x_total(ox, oz):
         zi = ZO.index(oz)
-        near_copy(0, zi).wait_recv()
-        near_copy(1, zi).wait_recv()
-        mine = block(0, oz)
-        return mine[...].astype(F32) + xnear[zi].astype(F32) + xnear[NZ + zi].astype(F32)
-
-    def z_task(oz):
-        total = x_total(oz)
+        came = (near_copy(zi), xnear) if ox == 0 else (far_copy(zi), xfar)
+        came[0].wait_recv()
+        return block(ox, oz)[...].astype(F32) + came[1][zi].astype(F32)
+
+    def z_task(ox, oz):
+        total = x_total(ox, oz)
+        mine = block(ox, oz)
         if oz == 4:
-            block(0, oz)[...] = total.astype(BF16)
-            go(z_copy(0, 4))
-            go(z_copy(1, 4))
+            mine[...] = total.astype(BF16)
+            go(z_copy(ox, 0, 4))
+            go(z_copy(ox, 1, 4))
             return
         side = 0 if oz > 0 else 1
         k = abs(oz)
-        index = side * 4 + k
-        z_copy(side, k + 1).wait_recv()
+        index = (ox * 2 + side) * 4 + k
+        z_copy(ox, side, k + 1).wait_recv()
         if k == 3:
-            block(0, oz)[...] = total.astype(BF16)
-            mine = block(0, oz, side)
+            mine[...] = total.astype(BF16)
+            mine = block(ox, oz, side)
             got = znear[index, side * HALF : (side + 1) * HALF, :]
             mine[...] = (mine[...].astype(F32) + got.astype(F32)).astype(BF16)
         else:
-            block(0, oz)[...] = (total + znear[index].astype(F32)).astype(BF16)
-        go(z_copy(side, k))
+            mine[...] = (total + znear[index].astype(F32)).astype(BF16)
+        go(z_copy(ox, side, k))
+
+    def z_tasks(*offsets):
+        for oz in offsets:
+            for ox in (1, 0):
+                z_task(ox, oz)
+
+    def z_total(ox):
+        total = x_total(ox, 0)
+        for side in range(2):
+            z_copy(ox, side, 1).wait_recv()
+            total = total + znear[(ox * 2 + side) * 4].astype(F32)
+        return total
+
+    def x_last():
+        block(1, 0)[...] = z_total(1).astype(BF16)
+        go(last_copy())
 
     def z_final():
-        total = x_total(0)
-        z_copy(0, 1).wait_recv()
-        z_copy(1, 1).wait_recv()
-        total = total + znear[0].astype(F32) + znear[4].astype(F32)
+        total = z_total(0)
+        last_copy().wait_recv()
+        total = total + xnear[NZ].astype(F32)
         o_tokens[...] = total[:, :width].astype(BF16)
         by_expert = total[:, width:grad_width].astype(BF16)
         by_expert = dot(identity(LANES), by_expert, ((1,), (1,)))
@@ -507,25 +512,23 @@
 
     for mat in range(3):
         y_task(0, mat)
+    behind(ROUNDS - 1, False)
+    pair_sum(ROUNDS - 2)
     pair_sum(ROUNDS - 1)
     x_start()
     y_task(1, 0)
+    z_tasks(4)
     y_task(1, 1)
-    x_add(zi_order[:4])
+    z_tasks(3, -3)
     y_task(1, 2)
-    x_add(zi_order[4:])
+    z_tasks(2, -2)
     y_task(2, 0)
+    z_tasks(1, -1)
     y_task(2, 1)
-    z_task(4)
-    z_task(3)
-    z_task(-3)
+    x_last()
     y_task(2, 2)
-    z_task(2)
-    z_task(-2)
-    z_task(1)
-    z_task(-1)
+    z_final()
     y_task(3, 0)
-    z_final()
     y_task(3, 1)
     y_task(3, 2)
 
@@ -590,13 +593,15 @@
             pltpu.VMEM((2, picked, width), BF16),
             pltpu.VMEM((3, ff, picked), BF16),
             pltpu.VMEM((2, 2 * CROW, ff), BF16),
+            pltpu.VMEM((2, CTOK, CROW), BF16),
+            pltpu.VMEM((2 * CROW, LANES), BF16),
             pltpu.VMEM((2, slots, gw), BF16),
             pltpu.VMEM((slots, gw), BF16),
             pltpu.VMEM((6, ff // 2, part), BF16),
             pltpu.VMEM((18, ff // 2, part), BF16),
             pltpu.VMEM((NZ, tok, gw), BF16),
-            pltpu.VMEM((2 * NZ, tok, gw), BF16),
-            pltpu.VMEM((8, tok, gw), BF16),
+            pltpu.VMEM((NZ + 1, tok, gw), BF16),
+            pltpu.VMEM((16, tok, gw), BF16),
             dma((5,)),
             dma((4 * BLOCKS,)),
             dma((4 * BLOCKS,)),
@@ -607,10 +612,10 @@
             dma((18,)),
             dma((NZ,)),
             dma((NZ,)),
-            dma((2 * NZ,)),
-            dma((2 * NZ,)),
-            dma((8,)),
-            dma((8,)),
+            dma((NZ + 1,)),
+            dma((NZ + 1,)),
+            dma((16,)),
+            dma((16,)),
         ],
         compiler_params=pltpu.CompilerParams(
             collective_id=0, has_side_effects=True, vmem_limit_bytes=63 << 20

time: 141 us -> 131 us (0.929); the launches traced: 138 us -> 130 us
  Pallas kernels: 137 us -> 129 us
    pallas_call x1, Pallas kernels: 135 us -> 126 us  [shards(): pl.pallas_call(kernel, out_shape=(jax.ShapeDtypeStruct((tok, width), BF16...]
where the time goes in v3:
time: 131 us; the launch traced here: 130 us
  Pallas kernels  129 us (98%)
    pallas_call x1, Pallas kernels, shards(): pl.pallas_call(kernel, out_shape=(jax.ShapeDtypeStruct((tok, width), BF16...  126 us

profile of v3, /device:TPU:32, one launch (start us, length us, event | category | flops | bytes accessed | tf_op | source)
XLA Modules:
  0.0 129.5 jit_solution(10100778389828752967)
XLA Ops:
  0.6 126.4 %shard_map.110 = (bf16[32,2048]{1,0:T(8,128)(2,1)}, bf16[10,32]{1,0:T(8,128)(2,1)}, bf16[512,512]{1,0:T(8,128)(2,1)}, bf16[512,512]{1,0:T(8,128)(2,1)}, bf16[512,512]{1,0:T(8,128)(2,1)}) custom-call(bf16[32,2048]{1,0:T(8,128)(2,1)} %tokens.1, bf16[32,2048]{1,0:T(8,128)(2,1)} %grad_out.1, bf16[10,32]{1,0:T(8,128)(2,1)} %bitcast.13, s32[10,32]{1,0:T(8,128)} %bitcast.12, ...), custom_call_target="tpu_custom_call" | custom-call | tf_op jit(solution)/shard_map/pallas_call | solution.py:577
  127.0 2.3 %shard_map.111 = (bf16[32,2048]{1,0:T(8,128)(2,1)}, bf16[10,32]{1,0:T(8,128)(2,1)}, bf16[512,512]{1,0:T(8,128)(2,1)}, bf16[512,512]{1,0:T(8,128)(2,1)}, bf16[512,512]{1,0:T(8,128)(2,1)}) custom-call(bf16[32,2048]{1,0:T(8,128)(2,1)} %get-tuple-element.15.refs_0_, bf16[10,32]{1,0:T(8,128)(2,1)} %get-tuple-element.16.refs_1_, ...), custom_call_target="tpu_custom_call" | custom-call | tf_op jit(solution)/shard_map/pallas_call | solution.py:624

commit v4 on v3

--- a/solution.py
+++ b/solution.py
@@ -78,16 +78,23 @@
 def kernel(
     tokens,
     grad_out,
-    combine,
-    expert_ids,
+    combine_in,
+    ids_in,
     w_gate,
     w_up,
     w_down,
+    r_tokens,
+    r_combine,
+    r_gate,
+    r_up,
+    r_down,
     o_tokens,
     o_combine,
     o_gate,
     o_up,
     o_down,
+    combine,
+    expert_ids,
     buf,
     wg,
     wu,
@@ -105,6 +112,7 @@
     xnear,
     znear,
     in_sem,
+    out_sem,
     ag_send,
     ag_recv,
     core_send,
@@ -138,10 +146,6 @@
     y_prev = {"grp": (group + NG - 1) % NG}
     x_next, x_prev, z_next, z_prev = at(1, 0), at(-1, 0), at(0, 1), at(0, -1)
 
-    barrier = pltpu.get_barrier_semaphore()
-    for other in (sibling, x_next, x_prev, z_next, z_prev, y_next, y_prev):
-        pl.semaphore_signal(barrier, inc=1, device_id=other, device_id_type=MESH)
-
     loads = [
         pltpu.make_async_copy(tokens, buf.at[core, pl.ds(0, TOK), pl.ds(0, width)], in_sem.at[0]),
         pltpu.make_async_copy(
@@ -151,8 +155,17 @@
         pltpu.make_async_copy(w_up, wu, in_sem.at[3]),
         pltpu.make_async_copy(w_down, wd, in_sem.at[4]),
     ]
-    for load in loads:
+    narrow = [
+        pltpu.make_async_copy(combine_in, combine, in_sem.at[5]),
+        pltpu.make_async_copy(ids_in, expert_ids, in_sem.at[6]),
+    ]
+    for load in narrow + loads:
         load.start()
+    barrier = pltpu.get_barrier_semaphore()
+    for other in (sibling, x_next, x_prev, z_next, z_prev, y_next, y_prev):
+        pl.semaphore_signal(barrier, inc=1, device_id=other, device_id_type=MESH)
+    for load in narrow:
+        load.wait()
     top = expert_ids.shape[0]
     expert_iota = lax.broadcasted_iota(jnp.int32, (LANES, TOK), 0)
     weights = combine[...].astype(F32)
@@ -236,6 +249,19 @@
             device_id_type=MESH,
         )
 
+    def wait_block(step, i, inner):
+        slot = step * CHUNK + i
+        rows = pl.ds(pl.multiple_of(slot * TOK, TOK), TOK)
+        pltpu.make_async_remote_copy(
+            src_ref=buf.at[1 - core, rows],
+            dst_ref=buf.at[1 - core, rows],
+            send_sem=core_send.at[slot],
+            recv_sem=ag_recv.at[((1 - core) * BLOCKS + slot) * 2],
+            device_id=sibling,
+            device_id_type=MESH,
+        ).wait_recv()
+        return inner
+
     def ahead(step):
         rows = pl.ds(pl.multiple_of(step * CTOK, CTOK), CTOK)
         first = pl.multiple_of(step * 2 * CROW, 2 * CROW)
@@ -248,7 +274,10 @@
         base = (lax.broadcasted_iota(jnp.int32, (1, CTOK), 1) // TOK * CAP).astype(F32)
         place = lax.broadcasted_iota(jnp.int32, (CROW, CTOK), 0).astype(F32)
         weight_parts = []
-        for kind in range(2):
+        for turn in range(2):
+            kind = core if turn == 0 else 1 - core
+            if turn == 1:
+                lax.fori_loop(0, CHUNK, functools.partial(wait_block, step), 0)
             table = buf[kind, rows, 2 * width : 2 * width + LANES]
             weight_row = dot(pick, table, ((1,), (1,)))
             routed = jnp.where(weight_row > 0, 1.0, 0.0)
@@ -256,14 +285,14 @@
             target = jnp.where(routed[0:1] > 0, base + rank[0:1] - 1.0, -1.0)
             select = jnp.where(place == target, 1.0, 0.0)
             weight_parts.append(jnp.sum(select * weight_row[0:1], axis=1, keepdims=True))
-            back_select[kind] = select.T.astype(BF16)
+            back_select[turn] = select.T.astype(BF16)
             select = select.astype(BF16)
-            own = pl.ds(pl.multiple_of(first + kind * CROW, CROW), CROW)
+            own = pl.ds(pl.multiple_of(first + turn * CROW, CROW), CROW)
             for c in range(2 * NG):
                 cols = slice((c % NG) * part, (c % NG + 1) * part)
                 picked = dot(select, buf[kind, rows, c * part : (c + 1) * part])
                 rows_all[c // NG, own, cols] = picked.astype(BF16)
-            service(step, kind)
+            service(step, turn)
         weight = jnp.concatenate(weight_parts, axis=0)
 
         combine_grad = jnp.zeros((2 * CROW, 1), F32)
@@ -299,14 +328,16 @@
             row_grad = dot(pair[0], wg[cols, :], ((1,), (1,)))
             row_grad = row_grad + dot(pair[1], wu[cols, :], ((1,), (1,)))
             row_grad = row_grad.astype(BF16)
-            for kind in range(2):
-                mine = row_grad[kind * CROW : (kind + 1) * CROW]
-                grads[kind, rows, cols] = dot(back_select[kind], mine).astype(BF16)
+            for turn in range(2):
+                kind = core if turn == 0 else 1 - core
+                mine = row_grad[turn * CROW : (turn + 1) * CROW]
+                grads[kind, rows, cols] = dot(back_select[turn], mine).astype(BF16)
             if serving:
                 service(step, 4 + c)
-        for kind in range(2):
-            mine = spread[kind * CROW : (kind + 1) * CROW, :]
-            grads[kind, rows, width:grad_width] = dot(back_select[kind], mine).astype(BF16)
+        for turn in range(2):
+            kind = core if turn == 0 else 1 - core
+            mine = spread[turn * CROW : (turn + 1) * CROW, :]
+            grads[kind, rows, width:grad_width] = dot(back_select[turn], mine).astype(BF16)
         pair_copy(1 - core, rows, step).start()
 
     def pair_sum(step):
@@ -324,21 +355,6 @@
     def round_body(step, carry):
         for kind in range(2):
             serve_all(step, kind, ORDER[kind][:CHUNK])
-
-        def wait_block(i, inner):
-            slot = step * CHUNK + i
-            rows = pl.ds(pl.multiple_of(slot * TOK, TOK), TOK)
-            pltpu.make_async_remote_copy(
-                src_ref=buf.at[1 - core, rows],
-                dst_ref=buf.at[1 - core, rows],
-                send_sem=core_send.at[slot],
-                recv_sem=ag_recv.at[((1 - core) * BLOCKS + slot) * 2],
-                device_id=sibling,
-                device_id_type=MESH,
-            ).wait_recv()
-            return inner
-
-        lax.fori_loop(0, CHUNK, wait_block, 0)
 
         @pl.when(step == 0)
         def _():
@@ -376,6 +392,13 @@
         )
 
     y_sent = []
+    results = [
+        pltpu.make_async_copy(o_tokens, r_tokens, out_sem.at[0]),
+        pltpu.make_async_copy(o_combine, r_combine, out_sem.at[1]),
+        pltpu.make_async_copy(o_gate, r_gate, out_sem.at[2]),
+        pltpu.make_async_copy(o_up, r_up, out_sem.at[3]),
+        pltpu.make_async_copy(o_down, r_down, out_sem.at[4]),
+    ]
 
     def y_task(step, mat):
         for way in range(2):
@@ -402,6 +425,8 @@
                     o_up[:, cols] = term.T.astype(BF16)
                 else:
                     o_down[cols, :] = term.astype(BF16)
+        if step == NG - 1:
+            results[2 + mat].start()
 
     def rows_of(ox, oz):
         a, b = slot_of(0, ox, oz), slot_of(1, ox, oz)
@@ -509,6 +534,8 @@
             named = expert_ids[k : k + 1, :] == expert_iota
             value = jnp.sum(jnp.where(named, by_expert, 0.0), axis=0, keepdims=True)
             o_combine[k : k + 1, :] = value.astype(BF16)
+        results[0].start()
+        results[1].start()
 
     for mat in range(3):
         y_task(0, mat)
@@ -548,6 +575,8 @@
     lax.fori_loop(0, BLOCKS // CHUNK, pair_done, 0)
     for copy in y_sent + rs_sent:
         copy.wait_send()
+    for copy in results:
+        copy.wait()
 
 
 def hand_out(*refs):
@@ -572,7 +601,6 @@
     picked = 2 * ROUNDS * CROW
     gw = width + LANES
     any_spec = pl.BlockSpec(memory_space=pl.ANY)
-    vmem_spec = pl.BlockSpec(memory_space=pltpu.VMEM)
     dma = pltpu.SemaphoreType.DMA
     results = pl.pallas_call(
         kernel,
@@ -583,9 +611,16 @@
             jax.ShapeDtypeStruct((part, ff), BF16),
             jax.ShapeDtypeStruct((ff, part), BF16),
         ),
-        in_specs=[any_spec, any_spec, vmem_spec, vmem_spec, any_spec, any_spec, any_spec],
-        out_specs=[vmem_spec] * 5,
+        in_specs=[any_spec] * 7,
+        out_specs=[any_spec] * 5,
         scratch_shapes=[
+            pltpu.VMEM((tok, width), BF16),
+            pltpu.VMEM((top, tok), BF16),
+            pltpu.VMEM((part, ff), BF16),
+            pltpu.VMEM((part, ff), BF16),
+            pltpu.VMEM((ff, part), BF16),
+            pltpu.VMEM((top, tok), BF16),
+            pltpu.VMEM((top, tok), jnp.int32),
             pltpu.VMEM((2, slots, 2 * width + LANES), BF16),
             pltpu.VMEM((width, ff), BF16),
             pltpu.VMEM((width, ff), BF16),
@@ -602,6 +637,7 @@
             pltpu.VMEM((NZ, tok, gw), BF16),
             pltpu.VMEM((NZ + 1, tok, gw), BF16),
             pltpu.VMEM((16, tok, gw), BF16),
+            dma((7,)),
             dma((5,)),
             dma((4 * BLOCKS,)),
             dma((4 * BLOCKS,)),

time: 131 us -> 129 us (0.985)
  Pallas kernels: 129 us -> 126 us
    pallas_call x1, Pallas kernels: 126 us -> 124 us  [shards(): pl.pallas_call(kernel, out_shape=(jax.ShapeDtypeStruct((tok, width), BF16...]
where the time goes in v4:
time: 129 us; the launch traced here: 127 us
  Pallas kernels  126 us (98%)
    pallas_call x1, Pallas kernels, shards(): pl.pallas_call(kernel, out_shape=(jax.ShapeDtypeStruct((tok, width), BF16...  124 us

profile of v4, /device:TPU:32, one launch (start us, length us, event | category | flops | bytes accessed | tf_op | source)
XLA Modules:
  0.0 127.1 jit_solution(15582050920414026716)
XLA Ops:
  0.6 124.0 %shard_map.110 = (bf16[32,2048]{1,0:T(8,128)(2,1)}, bf16[10,32]{1,0:T(8,128)(2,1)}, bf16[512,512]{1,0:T(8,128)(2,1)}, bf16[512,512]{1,0:T(8,128)(2,1)}, bf16[512,512]{1,0:T(8,128)(2,1)}) custom-call(bf16[32,2048]{1,0:T(8,128)(2,1)} %tokens.1, bf16[32,2048]{1,0:T(8,128)(2,1)} %grad_out.1, bf16[10,32]{1,0:T(8,128)(2,1)} %bitcast.13, s32[10,32]{1,0:T(8,128)} %bitcast.12, ...), custom_call_target="tpu_custom_call" | custom-call | tf_op jit(solution)/shard_map/pallas_call | solution.py:605
  124.6 2.3 %shard_map.111 = (bf16[32,2048]{1,0:T(8,128)(2,1)}, bf16[10,32]{1,0:T(8,128)(2,1)}, bf16[512,512]{1,0:T(8,128)(2,1)}, bf16[512,512]{1,0:T(8,128)(2,1)}, bf16[512,512]{1,0:T(8,128)(2,1)}) custom-call(bf16[32,2048]{1,0:T(8,128)(2,1)} %get-tuple-element.15.refs_0_, bf16[10,32]{1,0:T(8,128)(2,1)} %get-tuple-element.16.refs_1_, ...), custom_call_target="tpu_custom_call" | custom-call | tf_op jit(solution)/shard_map/pallas_call | solution.py:660

commit v5 on v4

--- a/solution.py
+++ b/solution.py
@@ -402,8 +402,11 @@
 
     def y_task(step, mat):
         for way in range(2):
-            shift = NG - 1 - step if way == 0 else 1 + step
-            term = tile((group + shift) % NG, mat, way)
+            if step < NG - 1:
+                shift = NG - 1 - step if way == 0 else 1 + step
+                term = tile((group + shift) % NG, mat, way)
+            else:
+                term = ysend[way * 3 + mat].astype(F32)
             if step == 0:
                 source = ysend.at[way * 3 + mat]
                 source[...] = term.astype(BF16)
@@ -416,7 +419,8 @@
             if step < NG - 1:
                 copy = y_copy(source, step, way, mat)
                 copy.start()
-                y_sent.append(copy)
+                if step > 0:
+                    y_sent.append(copy)
             else:
                 cols = slice(way * fhalf, (way + 1) * fhalf)
                 if mat == 0:
@@ -427,6 +431,13 @@
                     o_down[cols, :] = term.astype(BF16)
         if step == NG - 1:
             results[2 + mat].start()
+
+    def own_terms():
+        for way in range(2):
+            for mat in range(3):
+                held = ysend.at[way * 3 + mat]
+                y_copy(held, 0, way, mat).wait_send()
+                held[...] = tile(group, mat, way).astype(BF16)
 
     def rows_of(ox, oz):
         a, b = slot_of(0, ox, oz), slot_of(1, ox, oz)
@@ -554,6 +565,7 @@
     y_task(2, 1)
     x_last()
     y_task(2, 2)
+    own_terms()
     z_final()
     y_task(3, 0)
     y_task(3, 1)

time: 129 us -> 128 us (level)
  no operation moved by 1% of the time
where the time goes in v5:
time: 128 us; the launch traced here: 126 us
  Pallas kernels  126 us (98%)
    pallas_call x1, Pallas kernels, shards(): pl.pallas_call(kernel, out_shape=(jax.ShapeDtypeStruct((tok, width), BF16...  123 us

profile of v5, /device:TPU:32, one launch (start us, length us, event | category | flops | bytes accessed | tf_op | source)
XLA Modules:
  0.0 126.4 jit_solution(17516509096115147285)
XLA Ops:
  0.6 123.2 %shard_map.110 = (bf16[32,2048]{1,0:T(8,128)(2,1)}, bf16[10,32]{1,0:T(8,128)(2,1)}, bf16[512,512]{1,0:T(8,128)(2,1)}, bf16[512,512]{1,0:T(8,128)(2,1)}, bf16[512,512]{1,0:T(8,128)(2,1)}) custom-call(bf16[32,2048]{1,0:T(8,128)(2,1)} %tokens.1, bf16[32,2048]{1,0:T(8,128)(2,1)} %grad_out.1, bf16[10,32]{1,0:T(8,128)(2,1)} %bitcast.13, s32[10,32]{1,0:T(8,128)} %bitcast.12, ...), custom_call_target="tpu_custom_call" | custom-call | tf_op jit(solution)/shard_map/pallas_call | solution.py:617
  123.9 2.3 %shard_map.111 = (bf16[32,2048]{1,0:T(8,128)(2,1)}, bf16[10,32]{1,0:T(8,128)(2,1)}, bf16[512,512]{1,0:T(8,128)(2,1)}, bf16[512,512]{1,0:T(8,128)(2,1)}, bf16[512,512]{1,0:T(8,128)(2,1)}) custom-call(bf16[32,2048]{1,0:T(8,128)(2,1)} %get-tuple-element.15.refs_0_, bf16[10,32]{1,0:T(8,128)(2,1)} %get-tuple-element.16.refs_1_, ...), custom_call_target="tpu_custom_call" | custom-call | tf_op jit(solution)/shard_map/pallas_call | solution.py:672
